TPU v7x, 32 devices: a whole 2x2x4 slice. The times are simulated.
32 devices in a mesh: seq: 16 (over z, y, x), wsh: 2 (over core).
Axes of the slice: x: 2, y: 2, z: 4, core: 2. Of those that a mesh axis runs over, the one named last changes fastest.
Arguments:
- tokens: float32 [4, 1024, 1024], P('wsh', 'seq'), may hold values from -6 to 6
- doc_start: int32 [4, 1024], P('wsh', 'seq'), may hold values from 0 to 1023, as said below
- cotangent: float32 [4, 1024, 1024], P('wsh', 'seq'), may hold values from -6 to 6
- mix_gain: float32 [1024], replicated, may hold values from 0.5 to 1.5
- in_proj: bfloat16 [1024, 3072], P(None, 'wsh'), may hold values from -0.1875 to 0.1875
- conv_taps: float32 [3, 1024], replicated, may hold values from -3 to 3
- mix_proj: bfloat16 [1024, 1024], P(None, 'wsh'), may hold values from -0.1875 to 0.1875
- ffn_gain_a: float32 [1024], replicated, may hold values from 0.5 to 1.5
- gate_a: bfloat16 [1024, 4608], P(None, 'wsh'), may hold values from -0.1875 to 0.1875
- up_a: bfloat16 [1024, 4608], P(None, 'wsh'), may hold values from -0.1875 to 0.1875
- down_a: bfloat16 [4608, 1024], P(None, 'wsh'), may hold values from -0.09375 to 0.09375
- attn_gain: float32 [1024], replicated, may hold values from 0.5 to 1.5
- query_proj: bfloat16 [1024, 1024], P(None, 'wsh'), may hold values from -0.1875 to 0.1875
- key_proj: bfloat16 [1024, 512], P(None, 'wsh'), may hold values from -0.1875 to 0.1875
- value_proj: bfloat16 [1024, 512], P(None, 'wsh'), may hold values from -0.1875 to 0.1875
- attn_proj: bfloat16 [1024, 1024], P(None, 'wsh'), may hold values from -1 to 1
- query_gain: float32 [64], replicated, may hold values from 0.5 to 1.5
- key_gain: float32 [64], replicated, may hold values from 0.5 to 1.5
- ffn_gain_b: float32 [1024], replicated, may hold values from 0.5 to 1.5
- gate_b: bfloat16 [1024, 4608], P(None, 'wsh'), may hold values from -0.1875 to 0.1875
- up_b: bfloat16 [1024, 4608], P(None, 'wsh'), may hold values from -0.1875 to 0.1875
- down_b: bfloat16 [4608, 1024], P(None, 'wsh'), may hold values from -0.09375 to 0.09375
Outputs:
- output: float32 [4, 1024, 1024], P('wsh', 'seq')
- tokens_grad: float32 [4, 1024, 1024], P('wsh', 'seq')
- mix_gain_grad: float32 [1024], replicated
- in_proj_grad: float32 [1024, 3072], P('seq', 'wsh')
- conv_taps_grad: float32 [3, 1024], replicated
- mix_proj_grad: float32 [1024, 1024], P('seq', 'wsh')
- ffn_gain_a_grad: float32 [1024], replicated
- gate_a_grad: float32 [1024, 4608], P('seq', 'wsh')
- up_a_grad: float32 [1024, 4608], P('seq', 'wsh')
- down_a_grad: float32 [4608, 1024], P('wsh', 'seq')
- attn_gain_grad: float32 [1024], replicated
- query_proj_grad: float32 [1024, 1024], P('seq', 'wsh')
- key_proj_grad: float32 [1024, 512], P('seq', 'wsh')
- value_proj_grad: float32 [1024, 512], P('seq', 'wsh')
- attn_proj_grad: float32 [1024, 1024], P('seq', 'wsh')
- query_gain_grad: float32 [64], replicated
- key_gain_grad: float32 [64], replicated
- ffn_gain_b_grad: float32 [1024], replicated
- gate_b_grad: float32 [1024, 4608], P('seq', 'wsh')
- up_b_grad: float32 [1024, 4608], P('seq', 'wsh')
- down_b_grad: float32 [4608, 1024], P('wsh', 'seq')
Inputs may be any that keep to these rules, and one draw needn't show every extreme that they name: `doc_start`: each entry is the position of the first token of its document: entries never fall along a sequence, each equals the one before it or its own position, and the first is 0. In each run of 2 consecutive sequences starting at sequence 0, one, which one varies, is a single document; in each of the others the last token begins a document of its own.
All inputs are finite; a program needn't handle non-finite values.
Results may differ from a plain program's by a relative error of at most 0.025.
Values may be sent and summed in bfloat16 or wider, within the bound.
No kernel may reach another device: no remote copies, remote signals or barrier semaphores. Data moves between devices by JAX's collectives and lax.ppermute only.
A program may use at most 640 MiB of HBM per device.

v0:
```python
from functools import partial
import math

import jax
import jax.numpy as jnp
from jax import lax
from jax.sharding import PartitionSpec as P

EPS = 1e-05
ROPE_BASE = 1000000.0
MASKED = -1e30


def shifted_2(block, axis, distance):
    devices = range(lax.axis_size(axis))
    route = [(i - distance, i) for i in devices if i - distance in devices]
    return lax.ppermute(block, axis, route)


def norm_rows(values, gain_vec):
    return values * lax.rsqrt(jnp.mean(values * values, axis=-1, keepdims=True) + EPS) * gain_vec


def rope_tables(positions, head_width):
    frequency = ROPE_BASE ** (-(jnp.arange(0, head_width, 2, dtype=jnp.float32) / head_width))
    angles = positions.astype(jnp.float32)[:, None] * frequency[None, :]
    angles = jnp.concatenate([angles, angles], axis=-1)
    return (jnp.cos(angles)[:, None, :], jnp.sin(angles)[:, None, :])


def rotate(values, cosine_part, sine_part):
    half_width = values.shape[-1] // 2
    turned = jnp.concatenate([-values[..., half_width:], values[..., :half_width]], axis=-1)
    return values * cosine_part + turned * sine_part


def product(left, right):
    return jnp.dot(left, right, preferred_element_type=jnp.float32)


def product_tn(left, right):
    return lax.dot_general(
        left, right, (((0,), (0,)), ((), ())), preferred_element_type=jnp.float32
    )


def product_nt(left, right):
    return lax.dot_general(
        left, right, (((1,), (1,)), ((), ())), preferred_element_type=jnp.float32
    )


def gated_unit(gate_val, up_val):
    return jax.nn.silu(gate_val) * up_val


def ffn_forward(residual, gain_vec, gate_weight, up_weight, down_weight):
    hidden_low = norm_rows(residual, gain_vec).astype(jnp.bfloat16)
    gate_val = product(hidden_low, gate_weight)
    up_val = product(hidden_low, up_weight)
    act_low = gated_unit(gate_val, up_val).astype(jnp.bfloat16)
    return (residual + product(act_low, down_weight), (hidden_low, gate_val, up_val, act_low))


def ffn_backward(residual, gain_vec, saved, gate_weight, up_weight, down_weight, grad_after):
    hidden_low, gate_val, up_val, act_low = saved
    grad_low = grad_after.astype(jnp.bfloat16)
    grad_down_t = product_tn(grad_low, act_low)
    grad_act = product_nt(grad_low, down_weight)
    _, pull_unit = jax.vjp(gated_unit, gate_val, up_val)
    grad_gate_val, grad_up_val = pull_unit(grad_act)
    gate_low = grad_gate_val.astype(jnp.bfloat16)
    up_low = grad_up_val.astype(jnp.bfloat16)
    grad_gate = product_tn(hidden_low, gate_low)
    grad_up = product_tn(hidden_low, up_low)
    grad_hidden = product_nt(gate_low, gate_weight) + product_nt(up_low, up_weight)
    _, pull_norm = jax.vjp(norm_rows, residual, gain_vec)
    grad_resid, grad_gain = pull_norm(grad_hidden)
    return (grad_after + grad_resid, grad_gate, grad_up, grad_down_t, grad_gain)


def shards(
    tokens,
    doc_start,
    cotangent,
    mix_gain,
    in_proj,
    conv_taps,
    mix_proj,
    ffn_gain_a,
    gate_a,
    up_a,
    down_a,
    attn_gain,
    query_proj,
    key_proj,
    value_proj,
    attn_proj,
    query_gain,
    key_gain,
    ffn_gain_b,
    gate_b,
    up_b,
    down_b,
):
    streams, seq_rows, model_width = tokens.shape
    head_width = query_gain.shape[0]
    num_heads = model_width // head_width
    shard_count = lax.axis_size("wsh")
    kv_width = key_proj.shape[1] * shard_count
    kv_count = kv_width // head_width
    per_group = num_heads // kv_count
    tap_count = conv_taps.shape[0]
    margin = tap_count - 1
    score_scale = head_width ** (-0.5)
    token_count = streams * seq_rows
    total_rows = seq_rows * lax.axis_size("seq")
    block_rows = math.gcd(512, total_rows)
    block_count = total_rows // block_rows
    positions = lax.axis_index("seq") * seq_rows + jnp.arange(seq_rows, dtype=jnp.int32)
    cosine_part, sine_part = rope_tables(positions, head_width)

    def fetch_mixer():
        return (
            lax.all_gather(in_proj, "wsh", axis=1, tiled=True),
            lax.all_gather(mix_proj, "wsh", axis=1, tiled=True),
            lax.all_gather(gate_a, "wsh", axis=1, tiled=True),
            lax.all_gather(up_a, "wsh", axis=1, tiled=True),
            lax.all_gather(down_a, "wsh", axis=1, tiled=True),
        )

    def fetch_attention():
        return (
            lax.all_gather(query_proj, "wsh", axis=1, tiled=True),
            lax.all_gather(key_proj, "wsh", axis=1, tiled=True),
            lax.all_gather(value_proj, "wsh", axis=1, tiled=True),
            lax.all_gather(attn_proj, "wsh", axis=1, tiled=True),
            lax.all_gather(gate_b, "wsh", axis=1, tiled=True),
            lax.all_gather(up_b, "wsh", axis=1, tiled=True),
            lax.all_gather(down_b, "wsh", axis=1, tiled=True),
        )

    def convolve(extended, taps_now):
        running = jnp.zeros_like(extended[:, margin:])
        for tap_index in range(tap_count):
            offset = margin - tap_index
            shifted = extended[:, tap_index : tap_index + seq_rows]
            allowed = (positions[None, :] - offset >= doc_start)[:, :, None]
            running = running + jnp.where(allowed, shifted, 0.0) * taps_now[tap_index]
        return running

    def head_map(raw_heads, gain_vec):
        return rotate(norm_rows(raw_heads, gain_vec), cosine_part, sine_part)

    def reduce_grads(grad_list):
        packed = jnp.concatenate(
            [grad_piece.reshape(model_width, shard_count, -1) for grad_piece in grad_list], axis=2
        )
        packed = lax.psum_scatter(
            packed.astype(jnp.bfloat16), "wsh", scatter_dimension=1, tiled=True
        ).astype(jnp.float32)
        packed = lax.psum_scatter(packed, "seq", scatter_dimension=0, tiled=True)
        results = []
        offset = 0
        for grad_piece in grad_list:
            span_cols = grad_piece.shape[1] // shard_count
            results.append(packed[:, 0, offset : offset + span_cols])
            offset = offset + span_cols
        return results

    w_in, w_mix, w_gate_a, w_up_a, w_down_a = fetch_mixer()
    flat_tokens = tokens.reshape(token_count, model_width)
    low_one = norm_rows(flat_tokens, mix_gain).astype(jnp.bfloat16)
    projected = product(low_one, w_in)
    b_part = projected[:, :model_width]
    c_part = projected[:, model_width : 2 * model_width]
    x_part = projected[:, 2 * model_width :]
    gated = (b_part * x_part).reshape(streams, seq_rows, model_width)
    edge_rows = shifted_2(gated[:, seq_rows - margin :, :], "seq", 1)
    extended = jnp.concatenate([edge_rows, gated], axis=1)
    mixed_conv = convolve(extended, conv_taps).reshape(token_count, model_width)
    mixer_low = (c_part * mixed_conv).astype(jnp.bfloat16)
    resid_one = flat_tokens + product(mixer_low, w_mix)
    resid_two, saved_a = ffn_forward(resid_one, ffn_gain_a, w_gate_a, w_up_a, w_down_a)
    w_query, w_key, w_value, w_attn, w_gate_b, w_up_b, w_down_b = fetch_attention()
    low_three = norm_rows(resid_two, attn_gain).astype(jnp.bfloat16)
    query_raw = product(low_three, w_query).reshape(streams, seq_rows, num_heads, head_width)
    key_raw = product(low_three, w_key).reshape(streams, seq_rows, kv_count, head_width)
    value_raw = product(low_three, w_value)
    query_low = head_map(query_raw, query_gain).astype(jnp.bfloat16)
    key_low = head_map(key_raw, key_gain).astype(jnp.bfloat16).reshape(streams, seq_rows, kv_width)
    value_low = value_raw.astype(jnp.bfloat16).reshape(streams, seq_rows, kv_width)
    grouped_query = query_low.reshape(streams, seq_rows, kv_count, per_group, head_width)

    def gather_kv():
        return (
            lax.all_gather(key_low, "seq", axis=1, tiled=True),
            lax.all_gather(value_low, "seq", axis=1, tiled=True),
        )

    keys_all, values_all = gather_kv()

    def block_scores(stream_index, key_block, key_first, span_rows):
        key_places = key_first + jnp.arange(span_rows, dtype=jnp.int32)
        logits = (
            jnp.einsum(
                "qkgd,lkd->kgql",
                grouped_query[stream_index],
                key_block.reshape(span_rows, kv_count, head_width),
                preferred_element_type=jnp.float32,
            )
            * score_scale
        )
        allowed = (key_places[None, :] >= doc_start[stream_index][:, None]) & (
            key_places[None, :] <= positions[:, None]
        )
        return (logits, allowed)

    def reaches(stream_index, key_first, span_rows):
        return (key_first <= positions[seq_rows - 1]) & (
            key_first + span_rows - 1 >= doc_start[stream_index, 0]
        )

    def sweep(stream_index, advance, initial):

        def visit_block(block_index, carried):
            key_first = block_index * block_rows
            return lax.cond(
                reaches(stream_index, key_first, block_rows),
                partial(advance, key_first=key_first),
                lambda unchanged: unchanged,
                carried,
            )

        return lax.fori_loop(0, block_count, visit_block, initial)

    def log_total(stream_index, key_source):

        def advance(carried, key_first):
            peak_old, total_exp = carried
            key_block = lax.dynamic_slice_in_dim(key_source[stream_index], key_first, block_rows, 0)
            logits, allowed = block_scores(stream_index, key_block, key_first, block_rows)
            peak_new = jnp.maximum(peak_old, jnp.max(jnp.where(allowed, logits, MASKED), axis=-1))
            fresh_exp = jnp.where(allowed, jnp.exp(logits - peak_new[..., None]), 0.0)
            return (
                peak_new,
                total_exp * jnp.exp(peak_old - peak_new) + jnp.sum(fresh_exp, axis=-1),
            )

        start_state = (
            jnp.full((kv_count, per_group, seq_rows), MASKED, jnp.float32),
            jnp.zeros((kv_count, per_group, seq_rows), jnp.float32),
        )
        peak_final, total_exp = sweep(stream_index, advance, start_state)
        return peak_final + jnp.log(total_exp)

    def attend_stream(stream_index, key_source, value_source, log_norm):

        def advance(carried, key_first):
            key_block = lax.dynamic_slice_in_dim(key_source[stream_index], key_first, block_rows, 0)
            value_block = lax.dynamic_slice_in_dim(
                value_source[stream_index], key_first, block_rows, 0
            )
            logits, allowed = block_scores(stream_index, key_block, key_first, block_rows)
            shares = jnp.where(allowed, jnp.exp(logits - log_norm[..., None]), 0.0).astype(
                jnp.bfloat16
            )
            return carried + jnp.einsum(
                "kgql,lkd->qkgd",
                shares,
                value_block.reshape(block_rows, kv_count, head_width),
                preferred_element_type=jnp.float32,
            )

        return sweep(
            stream_index,
            advance,
            jnp.zeros((seq_rows, kv_count, per_group, head_width), jnp.float32),
        )

    log_norms = [log_total(stream_index, keys_all) for stream_index in range(streams)]
    attended = jnp.stack(
        [
            attend_stream(stream_index, keys_all, values_all, log_norms[stream_index])
            for stream_index in range(streams)
        ],
        axis=0,
    )
    attn_low = attended.reshape(token_count, model_width).astype(jnp.bfloat16)
    resid_three = resid_two + product(attn_low, w_attn)
    output, saved_b = ffn_forward(resid_three, ffn_gain_b, w_gate_b, w_up_b, w_down_b)
    w_query, w_key, w_value, w_attn, w_gate_b, w_up_b, w_down_b = fetch_attention()
    keys_back, values_back = gather_kv()
    grad_out = cotangent.reshape(token_count, model_width)
    grad_three, grad_gate_b, grad_up_b, grad_down_tb, grad_gain_b = ffn_backward(
        resid_three, ffn_gain_b, saved_b, w_gate_b, w_up_b, w_down_b, grad_out
    )
    grad_attn_low = grad_three.astype(jnp.bfloat16)
    grad_attn = product_tn(attn_low, grad_attn_low)
    grad_heads_low = product_nt(grad_attn_low, w_attn).astype(jnp.bfloat16)
    grouped_grad = grad_heads_low.reshape(streams, seq_rows, kv_count, per_group, head_width)
    delta_all = jnp.transpose(
        jnp.sum(grouped_grad.astype(jnp.float32) * attended, axis=-1), (0, 2, 3, 1)
    )
    deltas = [delta_all[stream_index] for stream_index in range(streams)]

    def query_grad_stream(stream_index, log_norm, delta_row):

        def advance(carried, key_first):
            key_block = lax.dynamic_slice_in_dim(keys_back[stream_index], key_first, block_rows, 0)
            value_block = lax.dynamic_slice_in_dim(
                values_back[stream_index], key_first, block_rows, 0
            )
            logits, allowed = block_scores(stream_index, key_block, key_first, block_rows)
            shares = jnp.where(allowed, jnp.exp(logits - log_norm[..., None]), 0.0)
            grad_shares = jnp.einsum(
                "qkgd,lkd->kgql",
                grouped_grad[stream_index],
                value_block.reshape(block_rows, kv_count, head_width),
                preferred_element_type=jnp.float32,
            )
            grad_logits = (shares * (grad_shares - delta_row[..., None])).astype(jnp.bfloat16)
            return carried + jnp.einsum(
                "kgql,lkd->qkgd",
                grad_logits,
                key_block.reshape(block_rows, kv_count, head_width),
                preferred_element_type=jnp.float32,
            )

        return (
            sweep(
                stream_index,
                advance,
                jnp.zeros((seq_rows, kv_count, per_group, head_width), jnp.float32),
            )
            * score_scale
        )

    query_grads = jnp.stack(
        [
            query_grad_stream(stream_index, log_norms[stream_index], deltas[stream_index])
            for stream_index in range(streams)
        ],
        axis=0,
    )

    def key_side(stream_index, key_first, span_rows):
        key_block = lax.dynamic_slice_in_dim(keys_back[stream_index], key_first, span_rows, 0)
        value_block = lax.dynamic_slice_in_dim(values_back[stream_index], key_first, span_rows, 0)
        logits, allowed = block_scores(stream_index, key_block, key_first, span_rows)
        shares = jnp.where(allowed, jnp.exp(logits - log_norms[stream_index][..., None]), 0.0)
        grad_shares = jnp.einsum(
            "qkgd,lkd->kgql",
            grouped_grad[stream_index],
            value_block.reshape(span_rows, kv_count, head_width),
            preferred_element_type=jnp.float32,
        )
        grad_logits = (shares * (grad_shares - deltas[stream_index][..., None])).astype(
            jnp.bfloat16
        )
        grad_keys = (
            jnp.einsum(
                "kgql,qkgd->lkd",
                grad_logits,
                grouped_query[stream_index],
                preferred_element_type=jnp.float32,
            )
            * score_scale
        )
        grad_values = jnp.einsum(
            "kgql,qkgd->lkd",
            shares.astype(jnp.bfloat16),
            grouped_grad[stream_index],
            preferred_element_type=jnp.float32,
        )
        return jnp.concatenate(
            [grad_keys.reshape(span_rows, kv_width), grad_values.reshape(span_rows, kv_width)],
            axis=-1,
        )

    row_span = seq_rows * lax.axis_size("seq")
    sub_rows = math.gcd(512, row_span)
    sub_count = row_span // sub_rows

    def one_piece(piece_index):
        key_first = piece_index * sub_rows
        columns = []
        for stream_index in range(streams):
            columns.append(
                lax.cond(
                    reaches(stream_index, key_first, sub_rows),
                    partial(key_side, stream_index, span_rows=sub_rows),
                    lambda ignored: jnp.zeros((sub_rows, 2 * kv_width), jnp.float32),
                    key_first,
                )
            )
        return jnp.stack(columns, axis=1)

    stacked = lax.map(one_piece, jnp.arange(sub_count, dtype=jnp.int32))
    kv_terms = lax.psum_scatter(
        stacked.reshape(row_span, streams, 2 * kv_width), "seq", scatter_dimension=0, tiled=True
    )
    key_grads = jnp.transpose(kv_terms[:, :, :kv_width], (1, 0, 2)).reshape(
        streams, seq_rows, kv_count, head_width
    )
    value_grads = jnp.transpose(kv_terms[:, :, kv_width:], (1, 0, 2)).reshape(token_count, kv_width)
    _, pull_query = jax.vjp(head_map, query_raw, query_gain)
    grad_query_raw, grad_query_gain = pull_query(
        query_grads.reshape(streams, seq_rows, num_heads, head_width)
    )
    _, pull_key = jax.vjp(head_map, key_raw, key_gain)
    grad_key_raw, grad_key_gain = pull_key(key_grads)
    query_back_low = grad_query_raw.reshape(token_count, model_width).astype(jnp.bfloat16)
    key_back_low = grad_key_raw.reshape(token_count, kv_width).astype(jnp.bfloat16)
    value_back_low = value_grads.astype(jnp.bfloat16)
    grad_query = product_tn(low_three, query_back_low)
    grad_key = product_tn(low_three, key_back_low)
    grad_value = product_tn(low_three, value_back_low)
    grad_hidden_three = (
        product_nt(query_back_low, w_query)
        + product_nt(key_back_low, w_key)
        + product_nt(value_back_low, w_value)
    )
    _, pull_three = jax.vjp(norm_rows, resid_two, attn_gain)
    grad_resid_three, grad_attn_gain = pull_three(grad_hidden_three)
    grad_two = grad_three + grad_resid_three
    reduced_two = reduce_grads(
        [grad_query, grad_key, grad_value, grad_attn, grad_gate_b, grad_up_b, grad_down_tb]
    )
    w_in, w_mix, w_gate_a, w_up_a, w_down_a = fetch_mixer()
    grad_one, grad_gate_a, grad_up_a, grad_down_ta, grad_gain_a = ffn_backward(
        resid_one, ffn_gain_a, saved_a, w_gate_a, w_up_a, w_down_a, grad_two
    )
    grad_mix_low = grad_one.astype(jnp.bfloat16)
    grad_mix = product_tn(mixer_low, grad_mix_low)
    grad_mixer = product_nt(grad_mix_low, w_mix)
    grad_c_part = grad_mixer * mixed_conv
    grad_conv = (grad_mixer * c_part).reshape(streams, seq_rows, model_width)
    _, pull_conv = jax.vjp(convolve, extended, conv_taps)
    grad_extended, grad_taps = pull_conv(grad_conv)
    returned = shifted_2(grad_extended[:, :margin, :], "seq", -1)
    grad_gated = grad_extended[:, margin:, :] + jnp.concatenate(
        [jnp.zeros((streams, seq_rows - margin, model_width), jnp.float32), returned], axis=1
    )
    grad_gated = grad_gated.reshape(token_count, model_width)
    grad_proj_low = jnp.concatenate(
        [grad_gated * x_part, grad_c_part, grad_gated * b_part], axis=-1
    ).astype(jnp.bfloat16)
    grad_in = product_tn(low_one, grad_proj_low)
    grad_hidden_one = product_nt(grad_proj_low, w_in)
    _, pull_one = jax.vjp(norm_rows, flat_tokens, mix_gain)
    grad_tokens_norm, grad_mix_gain = pull_one(grad_hidden_one)
    tokens_grad = (grad_one + grad_tokens_norm).reshape(streams, seq_rows, model_width)
    reduced_one = reduce_grads([grad_in, grad_mix, grad_gate_a, grad_up_a, grad_down_ta])
    small_grads = lax.psum(
        (
            grad_mix_gain,
            grad_taps,
            grad_gain_a,
            grad_attn_gain,
            grad_query_gain,
            grad_key_gain,
            grad_gain_b,
        ),
        ("seq", "wsh"),
    )
    return (
        output.reshape(streams, seq_rows, model_width),
        tokens_grad,
        small_grads[0],
        reduced_one[0],
        small_grads[1],
        reduced_one[1],
        small_grads[2],
        reduced_one[2],
        reduced_one[3],
        reduced_one[4].T,
        small_grads[3],
        reduced_two[0],
        reduced_two[1],
        reduced_two[2],
        reduced_two[3],
        small_grads[4],
        small_grads[5],
        small_grads[6],
        reduced_two[4],
        reduced_two[5],
        reduced_two[6].T,
    )


def solution(mesh):
    in_specs = (
        P("wsh", "seq", None),
        P("wsh", "seq"),
        P("wsh", "seq", None),
        P(),
        P(None, "wsh"),
        P(),
        P(None, "wsh"),
        P(),
        P(None, "wsh"),
        P(None, "wsh"),
        P(None, "wsh"),
        P(),
        P(None, "wsh"),
        P(None, "wsh"),
        P(None, "wsh"),
        P(None, "wsh"),
        P(),
        P(),
        P(),
        P(None, "wsh"),
        P(None, "wsh"),
        P(None, "wsh"),
    )
    out_specs = (
        P("wsh", "seq", None),
        P("wsh", "seq", None),
        P(),
        P("seq", "wsh"),
        P(),
        P("seq", "wsh"),
        P(),
        P("seq", "wsh"),
        P("seq", "wsh"),
        P("wsh", "seq"),
        P(),
        P("seq", "wsh"),
        P("seq", "wsh"),
        P("seq", "wsh"),
        P("seq", "wsh"),
        P(),
        P(),
        P(),
        P("seq", "wsh"),
        P("seq", "wsh"),
        P("wsh", "seq"),
    )
    return jax.shard_map(shards, mesh=mesh, in_specs=in_specs, out_specs=out_specs, check_vma=False)
```

profile of v0, /device:TPU:10, one launch (start us, length us, event | category | flops | bytes accessed | tf_op | source)
XLA Modules:
  0.0 2143.1 jit_solution(14343119017093896498)
XLA Ops:
  14.3 13.5 all-gather.15.cloned.1.call-done
  43.4 22.2 %all-gather.19.cloned.1.call-done = bf16[1024,4608]{1,0:T(8,128)(2,1)} async-done(((bf16[1024,2304]{1,0:T(8,128)(2,1)}), bf16[1024,4608]{1,0:T(8,128)(2,1)}) %all-gather.19.cloned.1.call-update) | async-done | bytes 9437200 | tf_op jit(solution)/shard_map/all_gather | solution.py:127
  65.7 6.6 fusion.189
  72.3 17.8 all-gather.21.cloned.1.call-done
  90.1 7.7 multiply_convert_fusion.3
  97.8 16.7 all-gather.23.cloned.1.call-done
  120.7 5.5 all-gather.25.cloned.1.call-done
  129.7 8.2 all-gather.29.cloned.1.call-done
  145.7 5.6 all-gather.33.cloned.1.call-done
  160.8 55.3 %all-gather.27.cloned.1.call-done = bf16[2,1024,512]{2,0,1:T(2,128)(2,1)} async-done(((bf16[2,64,512]{2,0,1:T(2,128)(2,1)}), bf16[2,1024,512]{2,0,1:T(2,128)(2,1)}) %all-gather.27.cloned.1.call-update) | async-done | bytes 2097168 | tf_op jit(solution)/shard_map/all_gather | solution.py:198
  216.1 6.2 copy.318
  222.2 56.4 %all-gather.31.cloned.1.call-done = bf16[2,1024,512]{2,0,1:T(2,128)(2,1)} async-done(((bf16[2,64,512]{2,0,1:T(2,128)(2,1)}), bf16[2,1024,512]{2,0,1:T(2,128)(2,1)}) %all-gather.31.cloned.1.call-update) | async-done | bytes 2097168 | tf_op jit(solution)/shard_map/all_gather | solution.py:197
  283.4 8.4 while.134
  292.7 11.6 while.135
  295.1 6.7 conditional.19
  304.3 8.5 while.132
  313.7 11.4 while.133
  316.1 6.6 conditional.17
  336.0 6.6 fusion.192
  342.6 6.5 fusion.193
  349.1 14.3 all-gather.41.cloned.1.call-done
  363.4 9.8 multiply_convert_fusion.1
  373.2 7.7 fusion.194
  397.3 71.3 %while.138 = (s32[]{:T(128)}, f32[2,512,2,1024]{3,1,0,2:T(8,128)}, s32[2]{0:T(128)S(1)}, s32[64]{0:T(128)S(1)}, s32[2,64]{1,0:T(2,128)S(1)}, /*index=5*/bf16[2,1...) while((s32[]{:T(128)}, f32[2,512,2,1024]{3,1,0,2:T(8,128)}, ...), condition=%wide.region_42.43_spmd, body=%wide.region_37.0_spmd.sunk | while | flops 547030016 | bytes 92449384 | solution.py:399
  401.2 14.7 conditional.22
  416.5 14.9 conditional.23
  471.0 15.3 while.137
  473.6 10.3 conditional.21
  487.2 15.1 while.136
  489.6 10.3 conditional.20
  523.1 12.5 copy.363
  542.8 5.4 convolution_convert_fusion.1
  548.1 134.0 %reduce-scatter.6.cloned.1.call-done = f32[64,2,1024]{2,0,1:T(8,128)} async-done(((f32[1024,2,1024]{2,0,1:T(8,128)}), f32[64,2,1024]{2,0,1:T(8,128)}) %reduce-scatter.6.cloned.1.call-update) | async-done | bytes 524304 | tf_op jit(solution)/shard_map/reduce_scatter | solution.py:400
  694.6 7.9 bitcast_dynamic-update-slice_fusion.1
  702.5 7.9 bitcast_dynamic-update-slice_fusion
  710.4 7.9 constant_dynamic-update-slice_fusion.2
  725.6 11.5 multiply_convert_fusion
  740.3 9.3 multiply_reduce_fusion.7
  787.0 8.0 bitcast_dynamic-update-slice_fusion.4
  795.0 8.1 bitcast_dynamic-update-slice_fusion.3
  803.1 7.9 bitcast_dynamic-update-slice_fusion.2
  811.1 21.2 convert_element_type.267
  832.5 27.3 %reduce-scatter.8.cloned.1.call-done = bf16[1024,1,8960]{2,0,1:T(8,128)(2,1)} async-done(((bf16[1024,2,8960]{2,0,1:T(8,128)(2,1)}), bf16[1024,1,8960]{2,0,1:T(8,128)(2,1)}) %reduce-scatter.8.cloned.1.call-update) | async-done | bytes 18350096 | tf_op jit(solution)/shard_map/reduce_scatter | solution.py:159
  859.9 20.2 convert_element_type.266
  881.5 6.0 convolution_add_fusion.6
  892.9 44.9 %all-reduce.11 = (f32[1024]{0:T(1024)}, f32[3,1024]{1,0:T(4,128)}, f32[1024]{0:T(1024)}, f32[1024]{0:T(1024)}, f32[64]{0:T(128)}, /*index=5*/f32[64]{0:T(128)}, f32[1024]{0:T(1024)}) all-reduce(f32[1024]{0:T(1024)S(1)} %get-tuple-element.2573, f32[3,1024]{1,0:T(4,128)S(1)} %pad_add_fusion.4, ...), channel_id=1, replica_groups=mesh['seq'=16,'wsh'=2] {'seq','wsh'}, use_global_device_ids=true, to_apply=%region_49.50 | all-reduce | flops 7296 | bytes 58368 | tf_op jit(solution)/shard_map/psum | solution.py:455
  938.8 436.7 %reduce-scatter.14.cloned.1.call-done = f32[64,1,8448]{2,0,1:T(8,128)} async-done(((f32[1024,1,8448]{2,0,1:T(8,128)}), f32[64,1,8448]{2,0,1:T(8,128)}) %reduce-scatter.14.cloned.1.call-update) | async-done | bytes 2162704 | tf_op jit(solution)/shard_map/reduce_scatter | solution.py:162
  1381.4 749.0 %reduce-scatter.10.cloned.1.call-done = f32[64,1,8960]{2,0,1:T(8,128)} async-done(((f32[1024,1,8960]{2,0,1:T(8,128)}), f32[64,1,8960]{2,0,1:T(8,128)}) %reduce-scatter.10.cloned.1.call-update) | async-done | bytes 2293776 | tf_op jit(solution)/shard_map/reduce_scatter | solution.py:162
  (606 shorter events, 323.3 us)
Async XLA Ops:
  7.2 20.6 all-gather.15.cloned.1.call-start
  7.9 33.2 %all-gather.17.cloned.1.call-start = ((), (), s32[]{:S(2)}) async-start(), calls=%async_computation.6 | async-start | bytes 3145728 | tf_op jit(solution)/shard_map/all_gather | solution.py:126
  8.7 57.0 %all-gather.19.cloned.1.call-start = ((), (), s32[]{:S(2)}) async-start(), calls=%async_computation.7 | async-start | bytes 14155776 | tf_op jit(solution)/shard_map/all_gather | solution.py:127
  9.4 80.7 %all-gather.21.cloned.1.call-start = ((), (), s32[]{:S(2)}) async-start(), calls=%async_computation.8 | async-start | bytes 14155776 | tf_op jit(solution)/shard_map/all_gather | solution.py:128
  10.0 104.6 %all-gather.23.cloned.1.call-start = ((), (), s32[]{:S(2)}) async-start(), calls=%async_computation.9 | async-start | bytes 14155776 | tf_op jit(solution)/shard_map/all_gather | solution.py:129
  10.6 115.6 %all-gather.25.cloned.1.call-start = ((), (), s32[]{:S(2)}) async-start(), calls=%async_computation.10 | async-start | bytes 1572864 | tf_op jit(solution)/shard_map/all_gather | solution.py:136
  11.2 126.7 %all-gather.29.cloned.1.call-start = ((), (), s32[]{:S(2)}) async-start(), calls=%async_computation.12 | async-start | bytes 1572864 | tf_op jit(solution)/shard_map/all_gather | solution.py:135
  11.9 139.3 %all-gather.33.cloned.1.call-start = ((), (), s32[]{:S(2)}) async-start(), calls=%async_computation.14 | async-start | bytes 3145728 | tf_op jit(solution)/shard_map/all_gather | solution.py:134
  12.7 203.4 %all-gather.27.cloned.1.call-start = ((), (), s32[]{:S(2)}) async-start(), calls=%async_computation.11 | async-start | bytes 2228224 | tf_op jit(solution)/shard_map/all_gather | solution.py:198
  14.1 17.4 copy-start.126
  14.1 23.1 %copy-start.97 = (f32[1,1024]{1,0:T(1,128)}, f32[1,1024]{1,0:T(1,128)S(1)}, u32[]{:S(2)}) copy-start(f32[1,1024]{1,0:T(1,128)S(1)} %get-tuple-element.2765) | copy-start | bytes 12292
  14.2 23.1 %copy-start.99 = (f32[1,1024]{1,0:T(1,128)}, f32[1,1024]{1,0:T(1,128)S(1)}, u32[]{:S(2)}) copy-start(f32[1,1024]{1,0:T(1,128)S(1)} %get-tuple-element.2766) | copy-start | bytes 12292
  14.2 23.1 %copy-start.101 = (f32[1,1024]{1,0:T(1,128)}, f32[1,1024]{1,0:T(1,128)S(1)}, u32[]{:S(2)}) copy-start(f32[1,1024]{1,0:T(1,128)S(1)} %get-tuple-element.2767) | copy-start | bytes 12292
  14.3 20.7 copy-start.103
  31.7 5.6 collective-permute-start
  35.1 37.2 %copy-start.117 = (pred[2,64]{1,0:T(4,128)(4,1)}, pred[2,64]{1,0:T(4,128)(4,1)S(1)}, u32[]{:S(2)}) copy-start(pred[2,64]{1,0:T(4,128)(4,1)S(1)} %get-tuple-element.2774) | copy-start | bytes 388
  43.2 29.0 %copy-start.129 = (f32[128]{0:T(128)}, f32[128]{0:T(128)S(1)}, u32[]{:S(2)}) copy-start(f32[128]{0:T(128)S(1)} %get-tuple-element.2775) | copy-start | bytes 1540
  43.2 71.3 %copy-start.15 = (f32[128,1024]{1,0:T(8,128)}, f32[128,1024]{1,0:T(8,128)S(1)}, u32[]{:S(2)}) copy-start(f32[128,1024]{1,0:T(8,128)S(1)} %get-tuple-element.2776) | copy-start | bytes 1572868
  43.3 29.0 %copy-start.119 = (f32[128]{0:T(128)}, f32[128]{0:T(128)S(1)}, u32[]{:S(2)}) copy-start(f32[128]{0:T(128)S(1)} %fusion.176) | copy-start | bytes 1540
  43.4 46.7 %copy-start.44 = (bf16[128,1024]{1,0:T(8,128)(2,1)}, bf16[128,1024]{1,0:T(8,128)(2,1)S(1)}, u32[]{:S(2)}) copy-start(bf16[128,1024]{1,0:T(8,128)(2,1)S(1)} %multiply_convert_fusion.7) | copy-start | bytes 786436
  97.8 21.9 %copy-start.33 = (bf16[128,4608]{1,0:T(8,128)(2,1)}, bf16[128,4608]{1,0:T(8,128)(2,1)S(1)}, u32[]{:S(2)}) copy-start(bf16[128,4608]{1,0:T(8,128)(2,1)S(1)} %get-tuple-element.2777) | copy-start | bytes 3538948
  119.8 9.8 copy-start.121
  120.6 30.6 %copy-start.27 = (bf16[128,1024]{1,0:T(8,128)(2,1)}, bf16[128,1024]{1,0:T(8,128)(2,1)S(1)}, u32[]{:S(2)}) copy-start(bf16[128,1024]{1,0:T(8,128)(2,1)S(1)} %multiply_convert_fusion.6) | copy-start | bytes 786436
  128.5 150.2 %all-gather.31.cloned.1.call-start = ((), (), s32[]{:S(2)}) async-start(), calls=%async_computation.13 | async-start | bytes 2228224 | tf_op jit(solution)/shard_map/all_gather | solution.py:197
  128.8 30.1 %copy-start.75 = (f32[64,64]{1,0:T(8,128)}, f32[64,64]{1,0:T(8,128)S(1)}, u32[]{:S(2)}) copy-start(f32[64,64]{1,0:T(8,128)S(1)} %copy.309) | copy-start | bytes 49156
  129.4 29.5 %copy-start.73 = (f32[64,64]{1,0:T(8,128)}, f32[64,64]{1,0:T(8,128)S(1)}, u32[]{:S(2)}) copy-start(f32[64,64]{1,0:T(8,128)S(1)} %copy.307) | copy-start | bytes 49156
  142.5 189.8 %all-gather.35.cloned.1.call-start = ((), (), s32[]{:S(2)}) async-start(), calls=%async_computation.15 | async-start | bytes 3145728 | tf_op jit(solution)/shard_map/all_gather | solution.py:137
  143.2 192.8 %all-gather.37.cloned.1.call-start = ((), (), s32[]{:S(2)}) async-start(), calls=%async_computation.16 | async-start | bytes 14155776 | tf_op jit(solution)/shard_map/all_gather | solution.py:138
  143.8 198.8 %all-gather.39.cloned.1.call-start = ((), (), s32[]{:S(2)}) async-start(), calls=%async_computation.17 | async-start | bytes 14155776 | tf_op jit(solution)/shard_map/all_gather | solution.py:139
  144.6 218.8 %all-gather.41.cloned.1.call-start = ((), (), s32[]{:S(2)}) async-start(), calls=%async_computation.18 | async-start | bytes 14155776 | tf_op jit(solution)/shard_map/all_gather | solution.py:140
  145.2 537.0 %reduce-scatter.6.cloned.1.call-start = ((), (), s32[]{:S(2)}) async-start(), calls=%async_computation.19 | async-start | bytes 8912896 | tf_op jit(solution)/shard_map/reduce_scatter | solution.py:400
  145.6 217.7 %copy-start.66 = (bf16[128,1024]{1,0:T(8,128)(2,1)}, bf16[128,1024]{1,0:T(8,128)(2,1)S(1)}, u32[]{:S(2)}) copy-start(bf16[128,1024]{1,0:T(8,128)(2,1)S(1)} %bitcast_convert_fusion) | copy-start | bytes 786436
  468.7 342.4 %reduce-scatter.12.cloned.1.call-start = ((), (), s32[]{:S(2)}) async-start(), calls=%async_computation.22 | async-start | bytes 51904512 | tf_op jit(solution)/shard_map/reduce_scatter | solution.py:159
  523.1 12.6 copy-start.41
  542.8 140.5 %copy-start.76 = (f32[64,64]{1,0:T(8,128)S(1)}, f32[64,64]{1,0:T(8,128)}, u32[]{:S(2)}) copy-start(f32[64,64]{1,0:T(8,128)} %copy-done.75) | copy-start | bytes 49156
  718.3 141.6 %reduce-scatter.8.cloned.1.call-start = ((), (), s32[]{:S(2)}) async-start(), calls=%async_computation.20 | async-start | bytes 55050240 | tf_op jit(solution)/shard_map/reduce_scatter | solution.py:159
  723.3 13.8 slice-start
  725.6 11.6 slice-start.1
  725.6 11.6 slice-start.2
  740.3 9.3 copy-start.130
  740.3 9.5 copy-start.37
  740.3 9.5 copy-start.53
  754.9 23.9 %collective-permute-start.1 = (f32[2,2,1024]{2,1,0:T(2,128)}, f32[2,2,1024]{2,1,0:T(2,128)}, u32[]{:S(2)}, u32[]{:S(2)}) collective-permute-start(f32[2,2,1024]{2,1,0:T(2,128)} %pad_add_fusion.3), channel_id=1, source_target_pairs={{2,0},{4,2},{6,4},{8,6},{10,8},{12,10},{14,12},{16,14},{18,16},{20... | collective-permute-start | bytes 49160 | tf_op jit(solution)/shard_map/ppermute | solution.py:17
  811.0 564.5 %reduce-scatter.14.cloned.1.call-start = ((), (), s32[]{:S(2)}) async-start(), calls=%async_computation.23 | async-start | bytes 36765696 | tf_op jit(solution)/shard_map/reduce_scatter | solution.py:162
  832.3 1298.1 %reduce-scatter.10.cloned.1.call-start = ((), (), s32[]{:S(2)}) async-start(), calls=%async_computation.21 | async-start | bytes 38993920 | tf_op jit(solution)/shard_map/reduce_scatter | solution.py:162
  887.6 50.2 %copy-start.134 = (f32[128]{0:T(128)S(1)}, f32[128]{0:T(128)}, u32[]{:S(2)}) copy-start(f32[128]{0:T(128)} %copy-done.133) | copy-start | bytes 1540
  887.6 50.2 %copy-start.43 = (f32[128,1024]{1,0:T(8,128)S(1)}, f32[128,1024]{1,0:T(8,128)}, u32[]{:S(2)}) copy-start(f32[128,1024]{1,0:T(8,128)} %copy-done.42) | copy-start | bytes 1572868
  887.6 50.2 %copy-start.128 = (f32[128]{0:T(128)S(1)}, f32[128]{0:T(128)}, u32[]{:S(2)}) copy-start(f32[128]{0:T(128)} %copy-done.126) | copy-start | bytes 1540
  (111 other events, 346.9 us)
Sparse Core Ops, SparseCore 0:
  9.6 18.1 all-gather.14
  29.3 11.7 all-gather.16
  42.6 22.9 all-gather.18
  67.1 22.9 all-gather.20
  91.5 23.0 all-gather.22
  115.9 10.1 all-gather.24
  127.7 10.1 all-gather.28
  139.5 11.7 all-gather.32
  154.6 61.4 all-gather.26
  219.3 59.3 all-gather.30
  280.2 9.6 all-gather.34
  291.3 22.9 all-gather.36
  315.9 22.9 all-gather.38
  340.3 23.0 all-gather.40
  468.8 213.2 reduce-scatter.5
  718.4 45.4 reduce-scatter.11
  811.1 48.6 reduce-scatter.7
  865.9 509.5 reduce-scatter.13
  1377.9 752.4 reduce-scatter.9
where the time goes:
time: 2160 us; the launch traced here: 2140 us
  waiting for transfers between devices  1570 us (73%)
  local copies, waits for them, and re-layouts  218 us (10%)
  matrix products  180 us (8%)
  other arithmetic  80.5 us (4%)
  blocking collectives  44.9 us (2%)
  loops' own time  22 us (1%)
    reduce_scatter x2, waiting for transfers between devices, reduce_grads(): packed = lax.psum_scatter(packed, 'seq', scatter_dimension=0, tiled=True)  1190 us
    reduce_scatter x1, waiting for transfers between devices, shards(): lax.psum_scatter(stacked.reshape(row_span, streams, 2 * kv_width), 'seq',...  134 us
    all_gather x1, waiting for transfers between devices, gather_kv(): lax.all_gather(key_low, 'seq', axis=1, tiled=True)  56.4 us
    dot_general x12, matrix products, product_nt(): lax.dot_general(left, right, (((1,), (1,)), ((), ())), preferred_element_...  56.3 us
    all_gather x1, waiting for transfers between devices, gather_kv(): lax.all_gather(value_low, 'seq', axis=1, tiled=True)  55.3 us
    unnamed x266, local copies, waits for them, and re-layouts  53.6 us
    dot_general x12, matrix products, product(): return jnp.dot(left, right, preferred_element_type=jnp.float32)  52.2 us
    psum x1, blocking collectives, shards(): lax.psum((grad_mix_gain, grad_taps, grad_gain_a, grad_attn_gain, grad_que...  44.9 us
  transfers between devices with their start and end apart: 21, of which 16 were waited for; matrix products, arithmetic and copies ran while one was open for 15% of the time, Pallas kernels for 0%

commit v1 on v0

v1 whole, which is shorter than its diff:
```python
from functools import partial
import math

import jax
import jax.numpy as jnp
from jax import lax
from jax.experimental import pallas as pl
from jax.experimental.pallas import tpu as pltpu
from jax.sharding import Mesh, PartitionSpec as P

EPS = 1e-05
ROPE_BASE = 1000000.0
MASKED = -1e30
START_PEAK = -1e25
SEQ = ("z", "y", "x")
EVERY = ("z", "y", "x", "wsh")
SWAP = [(0, 1), (1, 0)]
BF16 = jnp.bfloat16
F32 = jnp.float32
LANES = 128


def norm_rows(values, gain_vec):
    return values * lax.rsqrt(jnp.mean(values * values, axis=-1, keepdims=True) + EPS) * gain_vec


def product(left, right):
    return jnp.dot(left, right, preferred_element_type=F32)


def product_tn(left, right):
    return lax.dot_general(left, right, (((0,), (0,)), ((), ())), preferred_element_type=F32)


def product_nt(left, right):
    return lax.dot_general(left, right, (((1,), (1,)), ((), ())), preferred_element_type=F32)


def gated_unit(gate_val, up_val):
    return jax.nn.silu(gate_val) * up_val


def swap_cores(block):
    return lax.ppermute(block, "wsh", SWAP)


def gather_cores(block, axis=0):
    return lax.all_gather(block, "wsh", axis=axis, tiled=True)


def half_of(array, which, axis=0):
    size = array.shape[axis] // 2
    return lax.dynamic_slice_in_dim(array, which * size, size, axis)


def ordered(core, own, other):
    first = jnp.where(core == 0, own, other)
    second = jnp.where(core == 0, other, own)
    return jnp.concatenate([first, second], axis=-1)


def lane_of(shape):
    return lax.broadcasted_iota(jnp.int32, shape, 1)


def two_heads(block):
    return jnp.concatenate([block[:, :64], block[:, 64:]], axis=0)


def side_by_side(block):
    rows = block.shape[0] // 2
    return jnp.concatenate([block[:rows], block[rows:]], axis=1)


def places(meta_ref, starts_ref, rows):
    block = pl.program_id(0)
    starts = starts_ref[...]
    starts = jnp.concatenate([starts, starts], axis=0)
    row = lax.broadcasted_iota(jnp.int32, (2 * rows, 1), 0)
    row = jnp.where(row >= rows, row - rows, row)
    mine = meta_ref[pl.num_programs(0)] + block * rows + row
    return starts, mine


def sweep_bounds(meta_ref, rows, span):
    block = pl.program_id(0)
    first = meta_ref[block] // span
    last = (meta_ref[pl.num_programs(0)] + (block + 1) * rows + span - 1) // span
    return first, last


def attend_kernel(meta_ref, query_ref, kv_ref, starts_ref, low_ref, full_ref, log_ref, *, span, scale):
    rows = query_ref.shape[0]
    query = two_heads(query_ref[...])
    starts, mine = places(meta_ref, starts_ref, rows)

    def advance(index, carried):
        peak, total, mixed = carried
        kv_block = kv_ref[pl.ds(pl.multiple_of(index * span, span), span), :]
        scores = product_nt(query, kv_block[:, :64]) * scale
        place = index * span + lane_of((1, span))
        scores = jnp.where((place >= starts) & (place <= mine), scores, MASKED)
        fresh_peak = jnp.maximum(peak, jnp.max(scores, axis=1, keepdims=True))
        shares = jnp.exp(scores - fresh_peak)
        keep = jnp.exp(peak - fresh_peak)
        total = total * keep + jnp.sum(shares, axis=1, keepdims=True)
        mixed = mixed * keep + product(shares.astype(BF16), kv_block[:, 64:])
        return fresh_peak, total, mixed

    first, last = sweep_bounds(meta_ref, rows, span)
    peak, total, mixed = lax.fori_loop(
        first,
        last,
        advance,
        (
            jnp.full((2 * rows, 1), START_PEAK, F32),
            jnp.zeros((2 * rows, 1), F32),
            jnp.zeros((2 * rows, 64), F32),
        ),
    )
    attended = side_by_side(mixed / total)
    low_ref[...] = attended.astype(BF16)
    full_ref[...] = attended
    log_ref[...] = side_by_side(jnp.broadcast_to(peak + jnp.log(total), (2 * rows, 64)))


def attend_back_kernel(
    meta_ref, query_ref, kv_ref, starts_ref, grad_ref, full_ref, log_ref, dq_ref, dkv_ref, sums_ref, *, span, scale
):
    rows = query_ref.shape[0]
    query = two_heads(query_ref[...])
    grad = two_heads(grad_ref[...])
    attended = two_heads(full_ref[...])
    logs = two_heads(log_ref[...])[:, :1]
    delta = jnp.sum(grad.astype(F32) * attended, axis=1, keepdims=True)
    starts, mine = places(meta_ref, starts_ref, rows)

    @pl.when(pl.program_id(0) == 0)
    def _():
        sums_ref[...] = jnp.zeros_like(sums_ref)

    def advance(index, query_grad):
        window = pl.ds(pl.multiple_of(index * span, span), span)
        kv_block = kv_ref[window, :]
        key, value = kv_block[:, :64], kv_block[:, 64:]
        scores = product_nt(query, key) * scale
        place = index * span + lane_of((1, span))
        scores = jnp.where((place >= starts) & (place <= mine), scores, MASKED)
        shares = jnp.exp(scores - logs)
        grad_scores = (shares * (product_nt(grad, value) - delta)).astype(BF16)
        key_grad = product_tn(grad_scores, query) * scale
        value_grad = product_tn(shares.astype(BF16), grad)
        sums_ref[window, :] += jnp.concatenate([key_grad, value_grad], axis=1)
        return query_grad + product(grad_scores, key)

    first, last = sweep_bounds(meta_ref, rows, span)
    query_grad = lax.fori_loop(first, last, advance, jnp.zeros((2 * rows, 64), F32))
    dq_ref[...] = side_by_side(query_grad * scale).astype(BF16)

    @pl.when(pl.program_id(0) == pl.num_programs(0) - 1)
    def _():
        dkv_ref[...] = sums_ref[...].astype(BF16)


def attend_blocks(length):
    return math.gcd(256, length)


def rows_spec(rows, columns, column_block=0):
    return pl.BlockSpec((rows, columns), lambda index: (index, column_block))


def whole_spec(rows, columns, column_block=0):
    return pl.BlockSpec((rows, columns), lambda index: (0, column_block))


SCALARS = pl.BlockSpec(memory_space=pltpu.SMEM)


def attend(meta, packed, kv, kv_block, starts, scale):
    length, keys = packed.shape[0], kv.shape[0]
    rows = attend_blocks(length)
    return pl.pallas_call(
        partial(attend_kernel, span=attend_blocks(keys), scale=scale),
        grid=(length // rows,),
        in_specs=[SCALARS, rows_spec(rows, LANES), whole_spec(keys, LANES, kv_block), rows_spec(rows, 1)],
        out_specs=[rows_spec(rows, LANES)] * 3,
        out_shape=[
            jax.ShapeDtypeStruct((length, LANES), BF16),
            jax.ShapeDtypeStruct((length, LANES), F32),
            jax.ShapeDtypeStruct((length, LANES), F32),
        ],
        compiler_params=pltpu.CompilerParams(vmem_limit_bytes=32 << 20),
        cost_estimate=pl.CostEstimate(flops=4 * length * keys * 64, bytes_accessed=2 << 20, transcendentals=length * keys),
    )(meta, packed, kv, starts)


def attend_back(meta, packed, kv, kv_block, starts, grad, full, logs, scale):
    length, keys = packed.shape[0], kv.shape[0]
    rows = attend_blocks(length)
    return pl.pallas_call(
        partial(attend_back_kernel, span=attend_blocks(keys), scale=scale),
        grid=(length // rows,),
        in_specs=[SCALARS, rows_spec(rows, LANES), whole_spec(keys, LANES, kv_block), rows_spec(rows, 1)]
        + [rows_spec(rows, LANES)] * 3,
        out_specs=[rows_spec(rows, LANES), whole_spec(keys, LANES)],
        out_shape=[jax.ShapeDtypeStruct((length, LANES), BF16), jax.ShapeDtypeStruct((keys, LANES), BF16)],
        scratch_shapes=[pltpu.VMEM((keys, LANES), F32)],
        compiler_params=pltpu.CompilerParams(vmem_limit_bytes=32 << 20),
        cost_estimate=pl.CostEstimate(flops=10 * length * keys * 64, bytes_accessed=3 << 20, transcendentals=length * keys),
    )(meta, packed, kv, starts, grad, full, logs)


def head_means(values):
    low_lanes = lane_of(values.shape) < 64
    low_mean = jnp.sum(jnp.where(low_lanes, values, 0.0), axis=1, keepdims=True) * (1.0 / 64)
    high_mean = jnp.sum(jnp.where(low_lanes, 0.0, values), axis=1, keepdims=True) * (1.0 / 64)
    return jnp.where(low_lanes, low_mean, high_mean)


def turn(values, sign):
    lower = (lane_of(values.shape) % 64) < 32
    return jnp.where(lower, -sign * pltpu.roll(values, LANES - 32, 1), sign * pltpu.roll(values, 32, 1))


def head_forward(raw, gain, cosine, sine):
    unit = raw * lax.rsqrt(head_means(raw * raw) + EPS) * gain
    return (unit * cosine + turn(unit, 1.0) * sine).astype(BF16)


def head_backward(raw, gain, cosine, sine, grad):
    back = grad * cosine + turn(grad * sine, -1.0)
    scale = lax.rsqrt(head_means(raw * raw) + EPS)
    gain_term = jnp.sum(back * raw * scale, axis=0, keepdims=True)
    back = back * gain
    raw_grad = back * scale - raw * (scale * scale * scale) * head_means(back * raw)
    return raw_grad.astype(BF16), gain_term


def heads_kernel(query_ref, key_ref, value_ref, cos_ref, sin_ref, query_gain_ref, key_gain_ref, out_ref):
    rows = out_ref.shape[1]
    groups = key_ref.shape[1] // 64
    sequences = query_ref.shape[0] // rows
    cosine, sine = cos_ref[...], sin_ref[...]
    for place in range(sequences):
        span = pl.ds(place * rows, rows)
        for pair in range(groups // 2):
            lanes = pl.ds(pair * LANES, LANES)
            key = head_forward(key_ref[span, lanes], key_gain_ref[...], cosine, sine)
            value = value_ref[span, lanes].astype(BF16)
            for side in range(2):
                group = 2 * pair + side
                query = head_forward(
                    query_ref[span, pl.ds(group * LANES, LANES)], query_gain_ref[...], cosine, sine
                )
                half = slice(64 * side, 64 * side + 64)
                out_ref[place * groups + group, :, 0:LANES] = query
                out_ref[place * groups + group, :, LANES : 2 * LANES] = jnp.concatenate(
                    [key[:, half], value[:, half]], axis=1
                )


def heads_back_kernel(
    grad_ref,
    query_ref,
    key_ref,
    cos_ref,
    sin_ref,
    query_gain_ref,
    key_gain_ref,
    dq_ref,
    dk_ref,
    dv_ref,
    query_term_ref,
    key_term_ref,
):
    rows = grad_ref.shape[1]
    groups = key_ref.shape[1] // 64
    sequences = query_ref.shape[0] // rows
    cosine, sine = cos_ref[...], sin_ref[...]
    query_term = jnp.zeros((1, LANES), F32)
    key_term = jnp.zeros((1, LANES), F32)
    for place in range(sequences):
        span = pl.ds(place * rows, rows)
        for pair in range(groups // 2):
            lanes = pl.ds(pair * LANES, LANES)
            sides = [grad_ref[place * groups + 2 * pair + side, :, LANES : 2 * LANES] for side in range(2)]
            key_grad = jnp.concatenate([sides[0][:, :64], sides[1][:, :64]], axis=1).astype(F32)
            dv_ref[span, lanes] = jnp.concatenate([sides[0][:, 64:], sides[1][:, 64:]], axis=1)
            low, term = head_backward(key_ref[span, lanes], key_gain_ref[...], cosine, sine, key_grad)
            dk_ref[span, lanes] = low
            key_term = key_term + term
            for side in range(2):
                group = 2 * pair + side
                wide = pl.ds(group * LANES, LANES)
                query_grad = grad_ref[place * groups + group, :, 0:LANES].astype(F32)
                low, term = head_backward(query_ref[span, wide], query_gain_ref[...], cosine, sine, query_grad)
                dq_ref[span, wide] = low
                query_term = query_term + term
    query_term_ref[...] = query_term
    key_term_ref[...] = key_term


def heads_forward(query, key, value, tables, query_gain, key_gain, rows):
    groups = key.shape[1] // 64
    blocks = query.shape[0] // rows * groups
    return pl.pallas_call(
        heads_kernel,
        out_shape=jax.ShapeDtypeStruct((blocks, rows, 2 * LANES), BF16),
        compiler_params=pltpu.CompilerParams(vmem_limit_bytes=32 << 20),
    )(query, key, value, *tables, query_gain, key_gain)


def heads_backward(grad, query, key, tables, query_gain, key_gain):
    return pl.pallas_call(
        heads_back_kernel,
        out_shape=[
            jax.ShapeDtypeStruct(query.shape, BF16),
            jax.ShapeDtypeStruct(key.shape, BF16),
            jax.ShapeDtypeStruct(key.shape, BF16),
            jax.ShapeDtypeStruct((1, LANES), F32),
            jax.ShapeDtypeStruct((1, LANES), F32),
        ],
        compiler_params=pltpu.CompilerParams(vmem_limit_bytes=32 << 20),
    )(grad, query, key, *tables, query_gain, key_gain)


class Reducer:
    def __init__(self):
        self.sizes = {name: lax.axis_size(name) for name in SEQ}
        self.paired = self.sizes["x"] == 2 and self.sizes["y"] == 2

    def exchange(self, block, axis):
        return lax.ppermute(block, axis, SWAP)

    def pick(self, columns, axis, which):
        owners = [self.sizes[name] for name in SEQ]
        shaped = columns.reshape(*owners, -1, columns.shape[-1])
        picked = lax.dynamic_index_in_dim(shaped, which, SEQ.index(axis), keepdims=False)
        return picked.reshape(-1, columns.shape[-1])

    def share_left(self, left, axis):
        turned = left.T
        if not self.paired:
            return turned
        place = lax.axis_index(axis)
        own = self.pick(turned, axis, place)
        return own, self.exchange(self.pick(turned, axis, 1 - place), axis)

    def share_right(self, right, axis):
        return (right, self.exchange(right, axis)) if self.paired else right

    def total(self, left, right, axis):
        if not self.paired:
            whole = product(left, right).astype(BF16)
            return lax.psum_scatter(whole, SEQ, scatter_dimension=0, tiled=True).astype(F32)
        other = "y" if axis == "x" else "x"
        place = lax.axis_index(other)

        def part(which):
            sums = 0.0
            for columns, values in zip(left, right):
                shaped = columns.reshape(self.sizes["z"], 2, -1, columns.shape[-1])
                picked = lax.dynamic_index_in_dim(shaped, which, 1, keepdims=False)
                sums = sums + product(picked.reshape(-1, columns.shape[-1]), values)
            return sums

        arrived = self.exchange(part(1 - place).astype(BF16), other)
        summed = (part(place) + arrived.astype(F32)).astype(BF16)
        return lax.psum_scatter(summed, "z", scatter_dimension=0, tiled=True).astype(F32)


def shards(
    tokens,
    doc_start,
    cotangent,
    mix_gain,
    in_proj,
    conv_taps,
    mix_proj,
    ffn_gain_a,
    gate_a,
    up_a,
    down_a,
    attn_gain,
    query_proj,
    key_proj,
    value_proj,
    attn_proj,
    query_gain,
    key_gain,
    ffn_gain_b,
    gate_b,
    up_b,
    down_b,
):
    streams, seq_rows, width = tokens.shape
    core = lax.axis_index("wsh")
    sequences = streams * lax.axis_size("wsh")
    token_count = streams * seq_rows
    head_width = query_gain.shape[0]
    groups = key_proj.shape[1] // head_width
    score_scale = head_width ** (-0.5)
    margin = conv_taps.shape[0] - 1
    half_width = width // 2
    chips = lax.axis_size(SEQ)
    chip = lax.axis_index(SEQ)
    positions = chip * seq_rows + jnp.arange(seq_rows, dtype=jnp.int32)
    reducer = Reducer()

    frequency = ROPE_BASE ** (-(jnp.arange(0, head_width, 2, dtype=F32) / head_width))
    angles = positions.astype(F32)[:, None] * jnp.tile(frequency, 4)[None, :]
    tables = (jnp.cos(angles), jnp.sin(angles))
    query_gain_row = jnp.tile(query_gain, 2)[None, :]
    key_gain_row = jnp.tile(key_gain, 2)[None, :]

    def split_rows(weight):
        return half_of(weight, core), swap_cores(half_of(weight, 1 - core))

    def out_product(left, pieces):
        return ordered(core, product(left, pieces[0]), product(left, pieces[1]))

    def out_product_back(grad, pieces):
        own = half_of(grad, core, 1)
        other = half_of(grad, 1 - core, 1)
        return product_nt(own, pieces[0]) + product_nt(other, pieces[1])

    def sum_cores(partial_rows):
        return half_of(partial_rows, core) + swap_cores(half_of(partial_rows, 1 - core))

    starts_here = gather_cores(doc_start)
    in_low, in_mid, in_high = (in_proj[:, index * half_width : (index + 1) * half_width] for index in range(3))
    in_mid = swap_cores(in_mid)
    mix_pieces = split_rows(mix_proj)
    down_a_pieces = split_rows(down_a)
    attn_pieces = split_rows(attn_proj)
    down_b_pieces = split_rows(down_b)

    flat_tokens = tokens.reshape(token_count, width)
    low_one = gather_cores(norm_rows(flat_tokens, mix_gain).astype(BF16))
    part_low = product(low_one, in_low)
    part_mid = product(low_one, in_mid)
    part_high = product(low_one, in_high)
    factor = jnp.where(core == 0, part_low, part_high)
    c_part = jnp.where(core == 0, part_high, part_low)
    gated = (part_mid * factor).reshape(sequences, seq_rows, half_width)
    edge_rows = lax.ppermute(gated[:, seq_rows - margin :, :], SEQ, [(i, i + 1) for i in range(chips - 1)])
    extended = jnp.concatenate([edge_rows, gated], axis=1)
    taps_here = half_of(conv_taps, core, 1)

    def convolve(extended_rows, taps_now):
        running = jnp.zeros_like(extended_rows[:, margin:])
        for tap_index in range(margin + 1):
            offset = margin - tap_index
            shifted = extended_rows[:, tap_index : tap_index + seq_rows]
            allowed = (positions[None, :] - offset >= starts_here)[:, :, None]
            running = running + jnp.where(allowed, shifted, 0.0) * taps_now[tap_index]
        return running

    mixed_conv = convolve(extended, taps_here).reshape(-1, half_width)
    mixer_low = (c_part * mixed_conv).astype(BF16)
    resid_one = flat_tokens + sum_cores(out_product(mixer_low, mix_pieces))

    def ffn_forward(residual, gain_vec, gate_weight, up_weight, down_pieces):
        hidden_low = gather_cores(norm_rows(residual, gain_vec).astype(BF16))
        gate_val = product(hidden_low, gate_weight)
        up_val = product(hidden_low, up_weight)
        act_low = gated_unit(gate_val, up_val).astype(BF16)
        result = residual + sum_cores(out_product(act_low, down_pieces))
        return result, (hidden_low, gate_val, up_val, act_low)

    resid_two, saved_a = ffn_forward(resid_one, ffn_gain_a, gate_a, up_a, down_a_pieces)

    low_three = gather_cores(norm_rows(resid_two, attn_gain).astype(BF16))
    query_raw = product(low_three, query_proj)
    key_raw = product(low_three, key_proj)
    value_raw = product(low_three, value_proj)
    packed = heads_forward(query_raw, key_raw, value_raw, tables, query_gain_row, key_gain_row, seq_rows)

    team = SEQ if chips == sequences * groups else ("y", "x")
    rest = () if team == SEQ else ("z",)
    to_heads = partial(lax.all_to_all, axis_name=team, split_axis=0, concat_axis=0, tiled=True)
    packed = to_heads(packed).reshape(-1, 2 * LANES)
    length = packed.shape[0]
    team_starts = lax.all_gather(starts_here, team, axis=1, tiled=True)
    own_starts = lax.dynamic_index_in_dim(team_starts, lax.axis_index(team) // groups, 0, keepdims=False)
    first_place = lax.axis_index(rest) * length if rest else 0
    meta = jnp.append(own_starts[:: attend_blocks(length)], first_place).astype(jnp.int32)
    own_starts = own_starts[:, None]
    if rest:
        kv, kv_block = lax.all_gather(packed[:, LANES:], rest, axis=0, tiled=True), 0
    else:
        kv, kv_block = packed, 1
    attended_low, attended_full, logs = attend(meta, packed, kv, kv_block, own_starts, score_scale)

    def from_heads(block):
        back = to_heads(block.reshape(sequences * groups, seq_rows, -1))
        back = back.reshape(sequences, groups, seq_rows, -1)
        return jnp.transpose(back, (0, 2, 1, 3)).reshape(sequences * seq_rows, -1)

    attn_low = from_heads(attended_low)
    resid_three = resid_two + sum_cores(out_product(attn_low, attn_pieces))
    output, saved_b = ffn_forward(resid_three, ffn_gain_b, gate_b, up_b, down_b_pieces)

    def ffn_backward(residual, gain_vec, saved, gate_weight, up_weight, down_pieces, grad_after, axis):
        hidden_low, gate_val, up_val, act_low = saved
        other = "y" if axis == "x" else "x"
        grad_low = gather_cores(grad_after.astype(BF16))
        grad_act = out_product_back(grad_low, down_pieces)
        _, pull_unit = jax.vjp(gated_unit, gate_val, up_val)
        grad_gate_val, grad_up_val = pull_unit(grad_act)
        gate_low = grad_gate_val.astype(BF16)
        up_low = grad_up_val.astype(BF16)
        grad_hidden = sum_cores(product_nt(gate_low, gate_weight) + product_nt(up_low, up_weight))
        _, pull_norm = jax.vjp(norm_rows, residual, gain_vec)
        grad_resid, grad_gain = pull_norm(grad_hidden)
        left = reducer.share_left(hidden_low, axis)
        grad_gate = reducer.total(left, reducer.share_right(gate_low, axis), axis)
        grad_up = reducer.total(left, reducer.share_right(up_low, axis), axis)
        down_left = reducer.share_left(grad_low, other)
        grad_down = reducer.total(down_left, reducer.share_right(act_low, other), other)
        return grad_after + grad_resid, grad_gate, grad_up, grad_down.T, grad_gain

    grad_out = cotangent.reshape(token_count, width)
    grad_three, grad_gate_b, grad_up_b, grad_down_b, grad_gain_b = ffn_backward(
        resid_three, ffn_gain_b, saved_b, gate_b, up_b, down_b_pieces, grad_out, "x"
    )
    grad_attn_low = gather_cores(grad_three.astype(BF16))
    grad_heads_low = out_product_back(grad_attn_low, attn_pieces).astype(BF16)
    grad_heads = jnp.transpose(
        grad_heads_low.reshape(sequences, seq_rows, groups, LANES), (0, 2, 1, 3)
    ).reshape(sequences * groups, seq_rows, LANES)
    grad_heads = to_heads(grad_heads).reshape(length, LANES)
    query_grads, kv_grads = attend_back(
        meta, packed, kv, kv_block, own_starts, grad_heads, attended_full, logs, score_scale
    )
    if rest:
        kv_grads = lax.psum_scatter(kv_grads, rest, scatter_dimension=0, tiled=True)
    packed_grads = jnp.concatenate([query_grads, kv_grads], axis=1)
    packed_grads = to_heads(packed_grads.reshape(sequences * groups, seq_rows, 2 * LANES))
    query_back, key_back, value_back, query_term, key_term = heads_backward(
        packed_grads, query_raw, key_raw, tables, query_gain_row, key_gain_row
    )
    grad_hidden_three = sum_cores(
        product_nt(query_back, query_proj) + product_nt(key_back, key_proj) + product_nt(value_back, value_proj)
    )
    _, pull_three = jax.vjp(norm_rows, resid_two, attn_gain)
    grad_resid_three, grad_attn_gain = pull_three(grad_hidden_three)
    grad_two = grad_three + grad_resid_three

    attn_left = reducer.share_left(gather_cores(attn_low, 1), "y")
    grad_attn = reducer.total(attn_left, reducer.share_right(half_of(grad_attn_low, core, 1), "y"), "y")
    qkv_back = jnp.concatenate([query_back, key_back, value_back], axis=1)
    qkv_left = reducer.share_left(low_three, "y")
    grad_qkv = reducer.total(qkv_left, reducer.share_right(qkv_back, "y"), "y")

    grad_one, grad_gate_a, grad_up_a, grad_down_a, grad_gain_a = ffn_backward(
        resid_one, ffn_gain_a, saved_a, gate_a, up_a, down_a_pieces, grad_two, "y"
    )
    grad_mix_low = gather_cores(grad_one.astype(BF16))
    grad_mixer = out_product_back(grad_mix_low, mix_pieces)
    grad_c_part = grad_mixer * mixed_conv
    grad_conv = (grad_mixer * c_part).reshape(sequences, seq_rows, half_width)
    _, pull_conv = jax.vjp(convolve, extended, taps_here)
    grad_extended, grad_taps = pull_conv(grad_conv)
    returned = lax.ppermute(grad_extended[:, :margin, :], SEQ, [(i + 1, i) for i in range(chips - 1)])
    grad_gated = grad_extended[:, margin:, :] + jnp.concatenate(
        [jnp.zeros((sequences, seq_rows - margin, half_width), F32), returned], axis=1
    )
    grad_gated = grad_gated.reshape(-1, half_width)
    grad_factor = grad_gated * part_mid
    mid_low = (grad_gated * factor).astype(BF16)
    low_low = jnp.where(core == 0, grad_factor, grad_c_part).astype(BF16)
    high_low = jnp.where(core == 0, grad_c_part, grad_factor).astype(BF16)
    grad_hidden_one = sum_cores(
        product_nt(low_low, in_low) + product_nt(mid_low, in_mid) + product_nt(high_low, in_high)
    )
    _, pull_one = jax.vjp(norm_rows, flat_tokens, mix_gain)
    grad_tokens_norm, grad_mix_gain = pull_one(grad_hidden_one)
    tokens_grad = (grad_one + grad_tokens_norm).reshape(streams, seq_rows, width)

    mix_left = reducer.share_left(gather_cores(mixer_low, 1), "x")
    grad_mix = reducer.total(mix_left, reducer.share_right(half_of(grad_mix_low, core, 1), "x"), "x")
    proj_back = jnp.concatenate([low_low, swap_cores(mid_low), high_low], axis=1)
    in_left = reducer.share_left(low_one, "x")
    grad_in = reducer.total(in_left, reducer.share_right(proj_back, "x"), "x")

    grad_taps = lax.dynamic_update_slice_in_dim(jnp.zeros_like(conv_taps), grad_taps, core * half_width, 1)
    small = jnp.concatenate(
        [
            grad_mix_gain,
            grad_taps.reshape(-1),
            grad_gain_a,
            grad_attn_gain,
            grad_gain_b,
            query_term[0],
            key_term[0],
        ]
    )
    small = lax.psum(small, EVERY)
    taps_end = width + conv_taps.size
    heads_at = taps_end + 3 * width

    def head_gain(offset):
        both = small[offset : offset + LANES]
        return both[:head_width] + both[head_width:]

    query_columns, key_columns = query_proj.shape[1], key_proj.shape[1]
    return (
        output.reshape(streams, seq_rows, width),
        tokens_grad,
        small[:width],
        grad_in,
        small[width:taps_end].reshape(conv_taps.shape),
        grad_mix,
        small[taps_end : taps_end + width],
        grad_gate_a,
        grad_up_a,
        grad_down_a,
        small[taps_end + width : taps_end + 2 * width],
        grad_qkv[:, :query_columns],
        grad_qkv[:, query_columns : query_columns + key_columns],
        grad_qkv[:, query_columns + key_columns :],
        grad_attn,
        head_gain(heads_at),
        head_gain(heads_at + LANES),
        small[taps_end + 2 * width : taps_end + 3 * width],
        grad_gate_b,
        grad_up_b,
        grad_down_b,
    )


def chip_grid(chips):
    along_z = math.gcd(4, chips)
    side = math.isqrt(chips // along_z)
    return along_z, chips // along_z // side, side


def solution(mesh):
    cores = mesh.shape["wsh"]
    grid = Mesh(mesh.devices.reshape(*chip_grid(mesh.shape["seq"]), cores), EVERY)
    tokens_spec = P("wsh", SEQ, None)
    columns = P(None, "wsh")
    grads = P(SEQ, "wsh")
    in_specs = (
        tokens_spec,
        P("wsh", SEQ),
        tokens_spec,
        P(),
        columns,
        P(),
        columns,
        P(),
        columns,
        columns,
        columns,
        P(),
        columns,
        columns,
        columns,
        columns,
        P(),
        P(),
        P(),
        columns,
        columns,
        columns,
    )
    out_specs = (
        tokens_spec,
        tokens_spec,
        P(),
        grads,
        P(),
        grads,
        P(),
        grads,
        grads,
        P("wsh", SEQ),
        P(),
        grads,
        grads,
        grads,
        grads,
        P(),
        P(),
        P(),
        grads,
        grads,
        P("wsh", SEQ),
    )
    return jax.shard_map(shards, mesh=grid, in_specs=in_specs, out_specs=out_specs, check_vma=False)
```

time: 2160 us -> 675 us (0.31)
  waiting for transfers between devices: 1570 us -> 222 us
  local copies, waits for them, and re-layouts: 218 us -> 65.1 us
  starting transfers between devices: 7.22 us -> 72.1 us
  blocking collectives: 44.9 us -> 103 us
  matrix products: 180 us -> 128 us
  other arithmetic: 80.5 us -> 36.4 us
  loops' own time: 22 us -> 0 us
  Pallas kernels: 0 us -> 21.6 us
    reduce_scatter x5 -> x10, waiting for transfers between devices: 1350 us -> 0.02 us  [total(): lax.psum_scatter(summed, 'z', scatter_dimension=0, tiled=True).astype(F32)]
    all_gather x14 -> x0, waiting for transfers between devices: 218 us -> none  [the longest x1 56.4 us: gather_kv(): lax.all_gather(key_low, 'seq', axis=1, tiled=True)]
    ppermute x2 -> x44, waiting for transfers between devices: 2.2 us -> 218 us  [the longest x28 212 us: exchange(): return lax.ppermute(block, axis, SWAP)]
    all_gather x0 -> x12, blocking collectives: none -> 59.6 us  [the longest x1 33.4 us: shards(): team_starts = lax.all_gather(starts_here, team, axis=1, tiled=True)]
    unnamed x266 -> x297, local copies, waits for them, and re-layouts: 53.6 us -> 8.55 us
    all_to_all x0 -> x4, starting transfers between devices: none -> 34.7 us  [the longest x1 12.7 us: from_heads(): back = to_heads(block.reshape(sequences * groups, seq_rows, -1))]
    dot_general x38 -> x58, matrix products: 124 us -> 91.3 us  [product(): return jnp.dot(left, right, preferred_element_type=F32)]
    convert_element_type x14 -> x18, other arithmetic: 48.9 us -> 17.6 us  [the longest x7 12.1 us: total(): lax.psum_scatter(summed, 'z', scatter_dimension=0, tiled=True).astype(F32)]
  transfers between devices with their start and end apart: 21 -> 58, of which waited for: 16 -> 19; matrix products, arithmetic and copies ran while one was open for 15% -> 32% of each run, Pallas kernels for 0% -> 3%
where the time goes in v1:
time: 675 us; the launch traced here: 664 us
  waiting for transfers between devices  222 us (33%)
  matrix products  128 us (19%)
  blocking collectives  103 us (15%)
  starting transfers between devices  72.1 us (11%)
  local copies, waits for them, and re-layouts  65.1 us (10%)
  other arithmetic  36.4 us (5%)
  Pallas kernels  21.6 us (3%)
  between operations  16.8 us (2%)
    ppermute x28, waiting for transfers between devices, exchange(): return lax.ppermute(block, axis, SWAP)  212 us
    dot_general x58, matrix products, product(): return jnp.dot(left, right, preferred_element_type=F32)  91.3 us
    psum x1, blocking collectives, shards(): small = lax.psum(small, EVERY)  43 us
    dot_general x18, matrix products, product_nt(): lax.dot_general(left, right, (((1,), (1,)), ((), ())), preferred_element_...  36.6 us
    all_gather x1, blocking collectives, shards(): team_starts = lax.all_gather(starts_here, team, axis=1, tiled=True)  33.4 us
    ppermute x28, starting transfers between devices, exchange(): return lax.ppermute(block, axis, SWAP)  27.5 us
    all_gather x11, blocking collectives, gather_cores(): return lax.all_gather(block, 'wsh', axis=axis, tiled=True)  26.3 us
    dynamic_slice x16, local copies, waits for them, and re-layouts, part(): picked = lax.dynamic_index_in_dim(shaped, which, 1, keepdims=False)  15.7 us
  transfers between devices with their start and end apart: 58, of which 19 were waited for; matrix products, arithmetic and copies ran while one was open for 32% of the time, Pallas kernels for 3%

profile of v1, /device:TPU:10, one launch (start us, length us, event | category | flops | bytes accessed | tf_op | source)
XLA Modules:
  0.0 664.1 jit_solution(6361697506664589589)
XLA Ops:
  22.3 3.4 collective-permute-start.1
  30.3 3.2 constant_dynamic-slice_fusion.50
  35.4 3.2 all_gather.38
  38.5 4.0 fusion.126
  42.6 2.9 multiply_convert_fusion.3
  56.7 3.8 shard_map.373
  60.5 7.2 %all-to-all-start = ((bf16[16,64,256]{2,1,0:T(8,128)(2,1)}), bf16[16,64,256]{2,1,0:T(8,128)(2,1)S(1)}, u32[]{:S(2)}, u32[]{:S(2)}) async-start(bf16[16,64,256]{2,1,0:T(8,128)(2,1)} %shard_map.373), calls=%async_computation | async-start | bytes 1048576 | tf_op jit(solution)/shard_map/all_to_all | solution.py:483
  67.7 3.2 constant_dynamic-slice_fusion.47
  70.9 33.4 %all-gather.1 = s32[16,64,4]{1,2,0:T(4,128)S(1)} all-gather(s32[1,64,4]{1,2,0:T(4,128)S(1)} %bitcast.374), channel_id=1, replica_groups=mesh['z'=4,'y'=2,'x'=2,'wsh'=2] {'z','y','x'}, dimensions={0}, use_global_device_ids=true | all-gather | bytes 17408 | tf_op jit(solution)/shard_map/all_gather | solution.py:485
  116.4 6.5 shard_map.374
  124.4 12.7 %all-to-all-start.1 = ((bf16[16,64,128]{2,1,0:T(8,128)(2,1)}), bf16[16,64,128]{2,1,0:T(8,128)(2,1)}, u32[]{:S(2)}, u32[]{:S(2)}) async-start(bf16[16,64,128]{2,1,0:T(8,128)(2,1)} %bitcast.281), calls=%async_computation.1 | async-start | bytes 524288 | tf_op jit(solution)/shard_map/all_to_all | solution.py:497
  137.1 4.0 fusion.29
  170.3 3.9 fusion.130
  176.2 5.6 multiply_convert_fusion.1
  185.3 2.7 convolution_add_fusion.23
  208.0 6.1 all-to-all-start.2
  218.0 3.2 fusion.152
  222.7 3.3 all-to-all-done.2
  226.0 8.3 %shard_map.375 = (bf16[1024,128]{1,0:T(8,128)(2,1)S(1)}, bf16[1024,128]{1,0:T(8,128)(2,1)S(1)}) custom-call(s32[5]{0:T(128)S(1)} %pad_add_fusion.2.meta_ref, bf16[1024,256]{1,0:T(8,128)(2,1)S(1)} %bitcast.278, bf16[1024,256]{1,0:T(8,128)(2,1)S(1)} %bitcast.279, s32[1024,1]{1,0:T(8,128)S(1)} %get-tuple-element.68.starts_ref, bf16[1024,128]{1,0:T(8,128)(2,1)S(1)} %bitcast.280, ...), custom_call_target="tpu_custom_call" | custom-call | flops 671088640 | bytes 3145728 | tf_op jit(solution)/shard_map/pallas_call | solution.py:201
  235.2 8.8 %all-to-all-start.3 = ((bf16[16,64,256]{2,1,0:T(8,128)(2,1)}), bf16[16,64,256]{2,1,0:T(8,128)(2,1)S(1)}, u32[]{:S(2)}, u32[]{:S(2)}) async-start(bf16[16,64,256]{2,1,0:T(8,128)(2,1)} %bitcast.20), calls=%async_computation.3 | async-start | bytes 1048576 | tf_op jit(solution)/shard_map/all_to_all | solution.py:540
  250.0 6.1 collective-permute-done.35
  258.1 3.1 shard_map.376
  265.1 2.7 all_gather.44
  267.8 2.7 fusion.33
  270.6 5.3 multiply_convert_fusion
  278.7 2.7 convolution_add_fusion.22
  288.3 9.1 %collective-permute-done.32 = bf16[256,1024]{1,0:T(8,128)(2,1)S(1)} collective-permute-done((bf16[256,1024]{1,0:T(8,128)(2,1)S(1)}, bf16[256,1024]{1,0:T(8,128)(2,1)S(1)}, u32[]{:S(2)}, u32[]{:S(2)}) %collective-permute-start.32) | collective-permute-done | bytes 524320 | tf_op jit(solution)/shard_map/ppermute | solution.py:334
  298.7 2.8 fusion.15
  306.5 27.4 %collective-permute-done.21 = bf16[256,512]{1,0:T(8,128)(2,1)S(1)} collective-permute-done((bf16[256,512]{1,0:T(8,128)(2,1)S(1)}, bf16[256,512]{1,0:T(8,128)(2,1)S(1)}, u32[]{:S(2)}, u32[]{:S(2)}) %collective-permute-start.21) | collective-permute-done | bytes 262176 | tf_op jit(solution)/shard_map/ppermute | solution.py:334
  337.7 2.9 fusion.14
  342.5 2.7 fusion.13
  351.4 23.1 %collective-permute-done.38 = bf16[256,2304]{1,0:T(8,128)(2,1)} collective-permute-done((bf16[256,2304]{1,0:T(8,128)(2,1)}, bf16[256,2304]{1,0:T(8,128)(2,1)}, u32[]{:S(2)}, u32[]{:S(2)}) %collective-permute-start.38) | collective-permute-done | bytes 1179680 | tf_op jit(solution)/shard_map/ppermute | solution.py:334
  374.5 2.8 fusion.12
  381.5 20.4 %collective-permute-done.42 = bf16[256,2304]{1,0:T(8,128)(2,1)S(1)} collective-permute-done((bf16[256,2304]{1,0:T(8,128)(2,1)S(1)}, bf16[256,2304]{1,0:T(8,128)(2,1)S(1)}, u32[]{:S(2)}, u32[]{:S(2)}) %collective-permute-start.42) | collective-permute-done | bytes 1179680 | tf_op jit(solution)/shard_map/ppermute | solution.py:334
  410.4 25.3 %collective-permute-done.16 = bf16[512,256]{1,0:T(8,128)(2,1)S(1)} collective-permute-done((bf16[512,256]{1,0:T(8,128)(2,1)S(1)}, bf16[512,256]{1,0:T(8,128)(2,1)S(1)}, u32[]{:S(2)}, u32[]{:S(2)}) %collective-permute-start.16) | collective-permute-done | bytes 262176 | tf_op jit(solution)/shard_map/ppermute | solution.py:334
  441.1 2.9 fusion.16
  445.9 20.2 %collective-permute-done.27 = bf16[512,256]{1,0:T(8,128)(2,1)S(1)} collective-permute-done((bf16[512,256]{1,0:T(8,128)(2,1)S(1)}, bf16[512,256]{1,0:T(8,128)(2,1)S(1)}, u32[]{:S(2)}, u32[]{:S(2)}) %collective-permute-start.27) | collective-permute-done | bytes 262176 | tf_op jit(solution)/shard_map/ppermute | solution.py:334
  471.4 3.1 collective-permute-start.13
  474.7 3.5 collective-permute-done.13
  480.5 11.3 %collective-permute-done.29 = bf16[256,2304]{1,0:T(8,128)(2,1)S(1)} collective-permute-done((bf16[256,2304]{1,0:T(8,128)(2,1)S(1)}, bf16[256,2304]{1,0:T(8,128)(2,1)S(1)}, u32[]{:S(2)}, u32[]{:S(2)}) %collective-permute-start.29) | collective-permute-done | bytes 1179680 | tf_op jit(solution)/shard_map/ppermute | solution.py:334
  491.9 2.9 fusion.10
  505.4 21.8 %collective-permute-done.25 = bf16[256,2304]{1,0:T(8,128)(2,1)S(1)} collective-permute-done((bf16[256,2304]{1,0:T(8,128)(2,1)}, bf16[256,2304]{1,0:T(8,128)(2,1)S(1)}, u32[]{:S(2)}, u32[]{:S(2)}) %collective-permute-start.25) | collective-permute-done | bytes 1179680 | tf_op jit(solution)/shard_map/ppermute | solution.py:334
  529.4 14.7 %collective-permute-done.18 = bf16[256,1536]{1,0:T(8,128)(2,1)S(1)} collective-permute-done((bf16[256,1536]{1,0:T(8,128)(2,1)S(1)}, bf16[256,1536]{1,0:T(8,128)(2,1)S(1)}, u32[]{:S(2)}, u32[]{:S(2)}) %collective-permute-start.18) | collective-permute-done | bytes 786464 | tf_op jit(solution)/shard_map/ppermute | solution.py:334
  552.2 2.9 fusion.8
  555.4 3.2 fusion.139
  564.9 26.4 %collective-permute-done.24 = bf16[256,2304]{1,0:T(8,128)(2,1)S(1)} collective-permute-done((bf16[256,2304]{1,0:T(8,128)(2,1)S(1)}, bf16[256,2304]{1,0:T(8,128)(2,1)S(1)}, u32[]{:S(2)}, u32[]{:S(2)}) %collective-permute-start.24) | collective-permute-done | bytes 1179680 | tf_op jit(solution)/shard_map/ppermute | solution.py:334
  591.3 2.8 fusion.6
  594.1 43.0 %psum.7 = f32[7424]{0:T(1024)S(1)} all-reduce(f32[7424]{0:T(1024)S(1)} %constant_dynamic-update-slice_fusion.5), channel_id=1, replica_groups=mesh['z'=4,'y'=2,'x'=2,'wsh'=2] {'z','y','x','wsh'}, use_global_device_ids=true, to_apply=%region_15.16 | all-reduce | flops 7424 | bytes 59392 | tf_op jit(solution)/shard_map/psum | solution.py:600
  (600 shorter events, 220.0 us)
Async XLA Ops:
  9.7 9.9 %collective-permute-start = (bf16[1024,512]{1,0:T(8,128)(2,1)}, bf16[1024,512]{1,0:T(8,128)(2,1)}, u32[]{:S(2)}, u32[]{:S(2)}) collective-permute-start(bf16[1024,512]{1,0:T(8,128)(2,1)} %slice.85), channel_id=1, source_target_pairs={{0,1},{1,0},{2,3},{3,2},{4,5},{5,4},{6,7},{7,6},{8,9},{9,8},{10,11... | collective-permute-start | bytes 3145736 | tf_op jit(solution)/shard_map/ppermute | solution.py:44
  10.5 18.2 %collective-permute-start.2 = (bf16[512,512]{1,0:T(8,128)(2,1)}, bf16[512,512]{1,0:T(8,128)(2,1)}, u32[]{:S(2)}, u32[]{:S(2)}) collective-permute-start(bf16[512,512]{1,0:T(8,128)(2,1)} %constant_dynamic-slice_fusion.51), channel_id=1, source_target_pairs={{0,1},{1,0},{2,3},{3,2},{4,5},{5,4},{6,7},{7,6},{8,9},{9,8},{10,11... | collective-permute-start | bytes 1572872 | tf_op jit(solution)/shard_map/ppermute | solution.py:44
  33.5 12.8 %collective-permute-start.4 = (bf16[2304,512]{1,0:T(8,128)(2,1)}, bf16[2304,512]{1,0:T(8,128)(2,1)}, u32[]{:S(2)}, u32[]{:S(2)}) collective-permute-start(bf16[2304,512]{1,0:T(8,128)(2,1)} %constant_dynamic-slice_fusion.50), channel_id=1, source_target_pairs={{0,1},{1,0},{2,3},{3,2},{4,5},{5,4},{6,7},{7,6},{8,9},{9,8},{10,11... | collective-permute-start | bytes 7077896 | tf_op jit(solution)/shard_map/ppermute | solution.py:44
  50.9 99.3 %collective-permute-start.6 = (bf16[512,512]{1,0:T(8,128)(2,1)}, bf16[512,512]{1,0:T(8,128)(2,1)}, u32[]{:S(2)}, u32[]{:S(2)}) collective-permute-start(bf16[512,512]{1,0:T(8,128)(2,1)} %constant_dynamic-slice_fusion.48), channel_id=1, source_target_pairs={{0,1},{1,0},{2,3},{3,2},{4,5},{5,4},{6,7},{7,6},{8,9},{9,8},{10,11... | collective-permute-start | bytes 1572872 | tf_op jit(solution)/shard_map/ppermute | solution.py:44
  60.5 55.9 %all-to-all-start = ((bf16[16,64,256]{2,1,0:T(8,128)(2,1)}), bf16[16,64,256]{2,1,0:T(8,128)(2,1)S(1)}, u32[]{:S(2)}, u32[]{:S(2)}) async-start(bf16[16,64,256]{2,1,0:T(8,128)(2,1)} %shard_map.373), calls=%async_computation | async-start | bytes 1048576 | tf_op jit(solution)/shard_map/all_to_all | solution.py:483
  70.9 104.9 %collective-permute-start.8 = (bf16[2304,512]{1,0:T(8,128)(2,1)}, bf16[2304,512]{1,0:T(8,128)(2,1)}, u32[]{:S(2)}, u32[]{:S(2)}) collective-permute-start(bf16[2304,512]{1,0:T(8,128)(2,1)} %constant_dynamic-slice_fusion.47), channel_id=1, source_target_pairs={{0,1},{1,0},{2,3},{3,2},{4,5},{5,4},{6,7},{7,6},{8,9},{9,8},{10,11... | collective-permute-start | bytes 7077896 | tf_op jit(solution)/shard_map/ppermute | solution.py:44
  114.8 26.9 %collective-permute-start.19 = (bf16[512,256]{1,0:T(8,128)(2,1)}, bf16[512,256]{1,0:T(8,128)(2,1)}, u32[]{:S(2)}, u32[]{:S(2)}) collective-permute-start(bf16[512,256]{1,0:T(8,128)(2,1)} %bitcast.40), channel_id=1, source_target_pairs={{0,2},{2,0},{1,3},{3,1},{4,6},{6,4},{5,7},{7,5},{8,10},{10,8},{9,1... | collective-permute-start | bytes 786440 | tf_op jit(solution)/shard_map/ppermute | solution.py:334
  124.4 24.3 %all-to-all-start.1 = ((bf16[16,64,128]{2,1,0:T(8,128)(2,1)}), bf16[16,64,128]{2,1,0:T(8,128)(2,1)}, u32[]{:S(2)}, u32[]{:S(2)}) async-start(bf16[16,64,128]{2,1,0:T(8,128)(2,1)} %bitcast.281), calls=%async_computation.1 | async-start | bytes 524288 | tf_op jit(solution)/shard_map/all_to_all | solution.py:497
  147.2 8.1 %collective-permute-start.30 = (bf16[512,256]{1,0:T(8,128)(2,1)}, bf16[512,256]{1,0:T(8,128)(2,1)}, u32[]{:S(2)}, u32[]{:S(2)}) collective-permute-start(bf16[512,256]{1,0:T(8,128)(2,1)} %bitcast.65), channel_id=1, source_target_pairs={{0,4},{4,0},{1,5},{5,1},{2,6},{6,2},{3,7},{7,3},{8,12},{12,8},{9,1... | collective-permute-start | bytes 786440 | tf_op jit(solution)/shard_map/ppermute | solution.py:334
  153.1 12.5 %collective-permute-start.7 = (f32[128,1024]{1,0:T(8,128)}, f32[128,1024]{1,0:T(8,128)}, u32[]{:S(2)}, u32[]{:S(2)}) collective-permute-start(f32[128,1024]{1,0:T(8,128)} %fusion.64), channel_id=1, source_target_pairs={{0,1},{1,0},{2,3},{3,2},{4,5},{5,4},{6,7},{7,6},{8,9},{9,8},{10,11... | collective-permute-start | bytes 1572872 | tf_op jit(solution)/shard_map/ppermute | solution.py:44
  162.4 31.1 %collective-permute-start.33 = (bf16[512,256]{1,0:T(8,128)(2,1)S(1)}, bf16[512,256]{1,0:T(8,128)(2,1)S(1)}, u32[]{:S(2)}, u32[]{:S(2)}) collective-permute-start(bf16[512,256]{1,0:T(8,128)(2,1)S(1)} %bitcast.361), channel_id=1, source_target_pairs={{0,4},{4,0},{1,5},{5,1},{2,6},{6,2},{3,7},{7,3},{8,12},{12,8},{9,1... | collective-permute-start | bytes 786440 | tf_op jit(solution)/shard_map/ppermute | solution.py:334
  194.2 104.4 %collective-permute-start.39 = (bf16[256,2304]{1,0:T(8,128)(2,1)}, bf16[256,2304]{1,0:T(8,128)(2,1)}, u32[]{:S(2)}, u32[]{:S(2)}) collective-permute-start(bf16[256,2304]{1,0:T(8,128)(2,1)} %get-tuple-element.73), channel_id=1, source_target_pairs={{0,2},{2,0},{1,3},{3,1},{4,6},{6,4},{5,7},{7,5},{8,10},{10,8},{9,1... | collective-permute-start | bytes 3538952 | tf_op jit(solution)/shard_map/ppermute | solution.py:334
  208.0 18.0 %all-to-all-start.2 = ((bf16[16,64,128]{2,1,0:T(8,128)(2,1)}), bf16[16,64,128]{2,1,0:T(8,128)(2,1)S(1)}, u32[]{:S(2)}, u32[]{:S(2)}) async-start(bf16[16,64,128]{2,1,0:T(8,128)(2,1)} %bitcast.18), calls=%async_computation.2 | async-start | bytes 524288 | tf_op jit(solution)/shard_map/all_to_all | solution.py:533
  215.9 31.2 %collective-permute-start.36 = (bf16[512,256]{1,0:T(8,128)(2,1)}, bf16[512,256]{1,0:T(8,128)(2,1)}, u32[]{:S(2)}, u32[]{:S(2)}) collective-permute-start(bf16[512,256]{1,0:T(8,128)(2,1)} %bitcast.81), channel_id=1, source_target_pairs={{0,2},{2,0},{1,3},{3,1},{4,6},{6,4},{5,7},{7,5},{8,10},{10,8},{9,1... | collective-permute-start | bytes 786440 | tf_op jit(solution)/shard_map/ppermute | solution.py:334
  221.2 24.0 %collective-permute-start.34 = (bf16[256,512]{1,0:T(8,128)(2,1)}, bf16[256,512]{1,0:T(8,128)(2,1)}, u32[]{:S(2)}, u32[]{:S(2)}) collective-permute-start(bf16[256,512]{1,0:T(8,128)(2,1)} %constant_dynamic-slice_fusion.45), channel_id=1, source_target_pairs={{0,4},{4,0},{1,5},{5,1},{2,6},{6,2},{3,7},{7,3},{8,12},{12,8},{9,1... | collective-permute-start | bytes 786440 | tf_op jit(solution)/shard_map/ppermute | solution.py:334
  235.2 22.9 %all-to-all-start.3 = ((bf16[16,64,256]{2,1,0:T(8,128)(2,1)}), bf16[16,64,256]{2,1,0:T(8,128)(2,1)S(1)}, u32[]{:S(2)}, u32[]{:S(2)}) async-start(bf16[16,64,256]{2,1,0:T(8,128)(2,1)} %bitcast.20), calls=%async_computation.3 | async-start | bytes 1048576 | tf_op jit(solution)/shard_map/all_to_all | solution.py:540
  244.0 252.6 %reduce-scatter.23.cloned.1.call-start = ((), (), s32[]{:S(2)}) async-start(), calls=%async_computation.20 | async-start | bytes 327680 | tf_op jit(solution)/shard_map/reduce_scatter | solution.py:370
  246.5 9.6 %collective-permute-start.35 = (bf16[256,512]{1,0:T(8,128)(2,1)S(1)}, bf16[256,512]{1,0:T(8,128)(2,1)S(1)}, u32[]{:S(2)}, u32[]{:S(2)}) collective-permute-start(bf16[256,512]{1,0:T(8,128)(2,1)S(1)} %fusion.46), channel_id=1, source_target_pairs={{0,2},{2,0},{1,3},{3,1},{4,6},{6,4},{5,7},{7,5},{8,10},{10,8},{9,1... | collective-permute-start | bytes 786440 | tf_op jit(solution)/shard_map/ppermute | solution.py:334
  258.0 381.8 %reduce-scatter.21.cloned.1.call-start = ((), (), s32[]{:S(2)}) async-start(), calls=%async_computation.19 | async-start | bytes 655360 | tf_op jit(solution)/shard_map/reduce_scatter | solution.py:370
  262.8 19.3 %collective-permute-start.31 = (bf16[256,1024]{1,0:T(8,128)(2,1)S(1)}, bf16[256,1024]{1,0:T(8,128)(2,1)S(1)}, u32[]{:S(2)}, u32[]{:S(2)}) collective-permute-start(bf16[256,1024]{1,0:T(8,128)(2,1)S(1)} %constant_dynamic-update-slice_fusion.2), channel_id=1, source_target_pairs={{0,4},{4,0},{1,5},{5,1},{2,6},{6,2},{3,7},{7,3},{8,12},{12,8},{9,1... | collective-permute-start | bytes 1572872 | tf_op jit(solution)/shard_map/ppermute | solution.py:334
  282.6 14.8 %collective-permute-start.32 = (bf16[256,1024]{1,0:T(8,128)(2,1)S(1)}, bf16[256,1024]{1,0:T(8,128)(2,1)S(1)}, u32[]{:S(2)}, u32[]{:S(2)}) collective-permute-start(bf16[256,1024]{1,0:T(8,128)(2,1)S(1)} %fusion.39), channel_id=1, source_target_pairs={{0,2},{2,0},{1,3},{3,1},{4,6},{6,4},{5,7},{7,5},{8,10},{10,8},{9,1... | collective-permute-start | bytes 1572872 | tf_op jit(solution)/shard_map/ppermute | solution.py:334
  287.5 15.7 %collective-permute-start.20 = (bf16[256,512]{1,0:T(8,128)(2,1)S(1)}, bf16[256,512]{1,0:T(8,128)(2,1)}, u32[]{:S(2)}, u32[]{:S(2)}) collective-permute-start(bf16[256,512]{1,0:T(8,128)(2,1)S(1)} %constant_dynamic-slice_fusion.42), channel_id=1, source_target_pairs={{0,2},{2,0},{1,3},{3,1},{4,6},{6,4},{5,7},{7,5},{8,10},{10,8},{9,1... | collective-permute-start | bytes 786440 | tf_op jit(solution)/shard_map/ppermute | solution.py:334
  298.6 344.2 %reduce-scatter.13.cloned.1.call-start = ((), (), s32[]{:S(2)}) async-start(), calls=%async_computation.15 | async-start | bytes 327680 | tf_op jit(solution)/shard_map/reduce_scatter | solution.py:370
  301.5 36.2 %collective-permute-start.40 = (bf16[256,2304]{1,0:T(8,128)(2,1)}, bf16[256,2304]{1,0:T(8,128)(2,1)S(1)}, u32[]{:S(2)}, u32[]{:S(2)}) collective-permute-start(bf16[256,2304]{1,0:T(8,128)(2,1)} %fusion.15), channel_id=1, source_target_pairs={{0,4},{4,0},{1,5},{5,1},{2,6},{6,2},{3,7},{7,3},{8,12},{12,8},{9,1... | collective-permute-start | bytes 3538952 | tf_op jit(solution)/shard_map/ppermute | solution.py:334
  304.4 29.5 %collective-permute-start.21 = (bf16[256,512]{1,0:T(8,128)(2,1)S(1)}, bf16[256,512]{1,0:T(8,128)(2,1)S(1)}, u32[]{:S(2)}, u32[]{:S(2)}) collective-permute-start(bf16[256,512]{1,0:T(8,128)(2,1)S(1)} %fusion.45), channel_id=1, source_target_pairs={{0,4},{4,0},{1,5},{5,1},{2,6},{6,2},{3,7},{7,3},{8,12},{12,8},{9,1... | collective-permute-start | bytes 786440 | tf_op jit(solution)/shard_map/ppermute | solution.py:334
  305.1 37.4 %collective-permute-start.37 = (bf16[256,2304]{1,0:T(8,128)(2,1)}, bf16[256,2304]{1,0:T(8,128)(2,1)S(1)}, u32[]{:S(2)}, u32[]{:S(2)}) collective-permute-start(bf16[256,2304]{1,0:T(8,128)(2,1)} %get-tuple-element.74), channel_id=1, source_target_pairs={{0,2},{2,0},{1,3},{3,1},{4,6},{6,4},{5,7},{7,5},{8,10},{10,8},{9,1... | collective-permute-start | bytes 3538952 | tf_op jit(solution)/shard_map/ppermute | solution.py:334
  335.9 308.4 %reduce-scatter.27.cloned.1.call-start = ((), (), s32[]{:S(2)}) async-start(), calls=%async_computation.22 | async-start | bytes 1474560 | tf_op jit(solution)/shard_map/reduce_scatter | solution.py:370
  340.6 305.6 %reduce-scatter.25.cloned.1.call-start = ((), (), s32[]{:S(2)}) async-start(), calls=%async_computation.21 | async-start | bytes 1474560 | tf_op jit(solution)/shard_map/reduce_scatter | solution.py:370
  345.2 29.2 %collective-permute-start.38 = (bf16[256,2304]{1,0:T(8,128)(2,1)}, bf16[256,2304]{1,0:T(8,128)(2,1)}, u32[]{:S(2)}, u32[]{:S(2)}) collective-permute-start(bf16[256,2304]{1,0:T(8,128)(2,1)} %fusion.13), channel_id=1, source_target_pairs={{0,4},{4,0},{1,5},{5,1},{2,6},{6,2},{3,7},{7,3},{8,12},{12,8},{9,1... | collective-permute-start | bytes 3538952 | tf_op jit(solution)/shard_map/ppermute | solution.py:334
  347.6 32.5 %collective-permute-start.41 = (bf16[512,256]{1,0:T(8,128)(2,1)}, bf16[512,256]{1,0:T(8,128)(2,1)}, u32[]{:S(2)}, u32[]{:S(2)}) collective-permute-start(bf16[512,256]{1,0:T(8,128)(2,1)} %bitcast.89), channel_id=1, source_target_pairs={{0,4},{4,0},{1,5},{5,1},{2,6},{6,2},{3,7},{7,3},{8,12},{12,8},{9,1... | collective-permute-start | bytes 786440 | tf_op jit(solution)/shard_map/ppermute | solution.py:334
  348.3 53.6 %collective-permute-start.42 = (bf16[256,2304]{1,0:T(8,128)(2,1)S(1)}, bf16[256,2304]{1,0:T(8,128)(2,1)S(1)}, u32[]{:S(2)}, u32[]{:S(2)}) collective-permute-start(bf16[256,2304]{1,0:T(8,128)(2,1)S(1)} %copy-done.15), channel_id=1, source_target_pairs={{0,4},{4,0},{1,5},{5,1},{2,6},{6,2},{3,7},{7,3},{8,12},{12,8},{9,1... | collective-permute-start | bytes 3538952 | tf_op jit(solution)/shard_map/ppermute | solution.py:334
  377.3 270.7 %reduce-scatter.29.cloned.1.call-start = ((), (), s32[]{:S(2)}) async-start(), calls=%async_computation.23 | async-start | bytes 1474560 | tf_op jit(solution)/shard_map/reduce_scatter | solution.py:370
  404.6 36.5 %collective-permute-start.43 = (bf16[256,2304]{1,0:T(8,128)(2,1)}, bf16[256,2304]{1,0:T(8,128)(2,1)}, u32[]{:S(2)}, u32[]{:S(2)}) collective-permute-start(bf16[256,2304]{1,0:T(8,128)(2,1)} %fusion.17), channel_id=1, source_target_pairs={{0,2},{2,0},{1,3},{3,1},{4,6},{6,4},{5,7},{7,5},{8,10},{10,8},{9,1... | collective-permute-start | bytes 3538952 | tf_op jit(solution)/shard_map/ppermute | solution.py:334
  407.5 28.3 %collective-permute-start.16 = (bf16[512,256]{1,0:T(8,128)(2,1)S(1)}, bf16[512,256]{1,0:T(8,128)(2,1)S(1)}, u32[]{:S(2)}, u32[]{:S(2)}) collective-permute-start(bf16[512,256]{1,0:T(8,128)(2,1)S(1)} %bitcast.363), channel_id=1, source_target_pairs={{0,2},{2,0},{1,3},{3,1},{4,6},{6,4},{5,7},{7,5},{8,10},{10,8},{9,1... | collective-permute-start | bytes 786440 | tf_op jit(solution)/shard_map/ppermute | solution.py:334
  436.4 29.7 %collective-permute-start.28 = (bf16[256,2304]{1,0:T(8,128)(2,1)S(1)}, bf16[256,2304]{1,0:T(8,128)(2,1)}, u32[]{:S(2)}, u32[]{:S(2)}) collective-permute-start(bf16[256,2304]{1,0:T(8,128)(2,1)S(1)} %copy-done.13), channel_id=1, source_target_pairs={{0,2},{2,0},{1,3},{3,1},{4,6},{6,4},{5,7},{7,5},{8,10},{10,8},{9,1... | collective-permute-start | bytes 3538952 | tf_op jit(solution)/shard_map/ppermute | solution.py:334
  439.3 55.5 %collective-permute-start.22 = (bf16[512,256]{1,0:T(8,128)(2,1)}, bf16[512,256]{1,0:T(8,128)(2,1)}, u32[]{:S(2)}, u32[]{:S(2)}) collective-permute-start(bf16[512,256]{1,0:T(8,128)(2,1)} %bitcast.48), channel_id=1, source_target_pairs={{0,4},{4,0},{1,5},{5,1},{2,6},{6,2},{3,7},{7,3},{8,12},{12,8},{9,1... | collective-permute-start | bytes 786440 | tf_op jit(solution)/shard_map/ppermute | solution.py:334
  444.0 205.8 %reduce-scatter.19.cloned.1.call-start = ((), (), s32[]{:S(2)}) async-start(), calls=%async_computation.18 | async-start | bytes 1474560 | tf_op jit(solution)/shard_map/reduce_scatter | solution.py:370
  444.3 21.8 %collective-permute-start.27 = (bf16[512,256]{1,0:T(8,128)(2,1)S(1)}, bf16[512,256]{1,0:T(8,128)(2,1)S(1)}, u32[]{:S(2)}, u32[]{:S(2)}) collective-permute-start(bf16[512,256]{1,0:T(8,128)(2,1)S(1)} %bitcast.362), channel_id=1, source_target_pairs={{0,2},{2,0},{1,3},{3,1},{4,6},{6,4},{5,7},{7,5},{8,10},{10,8},{9,1... | collective-permute-start | bytes 786440 | tf_op jit(solution)/shard_map/ppermute | solution.py:334
  468.2 23.7 %collective-permute-start.29 = (bf16[256,2304]{1,0:T(8,128)(2,1)S(1)}, bf16[256,2304]{1,0:T(8,128)(2,1)S(1)}, u32[]{:S(2)}, u32[]{:S(2)}) collective-permute-start(bf16[256,2304]{1,0:T(8,128)(2,1)S(1)} %fusion.11), channel_id=1, source_target_pairs={{0,4},{4,0},{1,5},{5,1},{2,6},{6,2},{3,7},{7,3},{8,12},{12,8},{9,1... | collective-permute-start | bytes 3538952 | tf_op jit(solution)/shard_map/ppermute | solution.py:334
  480.4 20.2 %collective-permute-start.17 = (bf16[256,1536]{1,0:T(8,128)(2,1)S(1)}, bf16[256,1536]{1,0:T(8,128)(2,1)S(1)}, u32[]{:S(2)}, u32[]{:S(2)}) collective-permute-start(bf16[256,1536]{1,0:T(8,128)(2,1)S(1)} %pad_maximum_fusion), channel_id=1, source_target_pairs={{0,2},{2,0},{1,3},{3,1},{4,6},{6,4},{5,7},{7,5},{8,10},{10,8},{9,1... | collective-permute-start | bytes 2359304 | tf_op jit(solution)/shard_map/ppermute | solution.py:334
  494.8 156.9 %reduce-scatter.11.cloned.1.call-start = ((), (), s32[]{:S(2)}) async-start(), calls=%async_computation.14 | async-start | bytes 983040 | tf_op jit(solution)/shard_map/reduce_scatter | solution.py:370
  498.1 29.1 %collective-permute-start.25 = (bf16[256,2304]{1,0:T(8,128)(2,1)}, bf16[256,2304]{1,0:T(8,128)(2,1)S(1)}, u32[]{:S(2)}, u32[]{:S(2)}) collective-permute-start(bf16[256,2304]{1,0:T(8,128)(2,1)} %get-tuple-element.71), channel_id=1, source_target_pairs={{0,4},{4,0},{1,5},{5,1},{2,6},{6,2},{3,7},{7,3},{8,12},{12,8},{9,1... | collective-permute-start | bytes 3538952 | tf_op jit(solution)/shard_map/ppermute | solution.py:334
  501.5 42.5 %collective-permute-start.18 = (bf16[256,1536]{1,0:T(8,128)(2,1)S(1)}, bf16[256,1536]{1,0:T(8,128)(2,1)S(1)}, u32[]{:S(2)}, u32[]{:S(2)}) collective-permute-start(bf16[256,1536]{1,0:T(8,128)(2,1)S(1)} %fusion.19), channel_id=1, source_target_pairs={{0,4},{4,0},{1,5},{5,1},{2,6},{6,2},{3,7},{7,3},{8,12},{12,8},{9,1... | collective-permute-start | bytes 2359304 | tf_op jit(solution)/shard_map/ppermute | solution.py:334
  504.7 58.1 %collective-permute-start.23 = (bf16[256,2304]{1,0:T(8,128)(2,1)}, bf16[256,2304]{1,0:T(8,128)(2,1)}, u32[]{:S(2)}, u32[]{:S(2)}) collective-permute-start(bf16[256,2304]{1,0:T(8,128)(2,1)} %get-tuple-element.72), channel_id=1, source_target_pairs={{0,4},{4,0},{1,5},{5,1},{2,6},{6,2},{3,7},{7,3},{8,12},{12,8},{9,1... | collective-permute-start | bytes 3538952 | tf_op jit(solution)/shard_map/ppermute | solution.py:334
  528.7 23.5 %collective-permute-start.26 = (bf16[256,2304]{1,0:T(8,128)(2,1)}, bf16[256,2304]{1,0:T(8,128)(2,1)}, u32[]{:S(2)}, u32[]{:S(2)}) collective-permute-start(bf16[256,2304]{1,0:T(8,128)(2,1)} %fusion.9), channel_id=1, source_target_pairs={{0,2},{2,0},{1,3},{3,1},{4,6},{6,4},{5,7},{7,5},{8,10},{10,8},{9,1... | collective-permute-start | bytes 3538952 | tf_op jit(solution)/shard_map/ppermute | solution.py:334
  545.4 108.0 %reduce-scatter.17.cloned.1.call-start = ((), (), s32[]{:S(2)}) async-start(), calls=%async_computation.17 | async-start | bytes 1474560 | tf_op jit(solution)/shard_map/reduce_scatter | solution.py:370
  555.2 100.0 %reduce-scatter.15.cloned.1.call-start = ((), (), s32[]{:S(2)}) async-start(), calls=%async_computation.16 | async-start | bytes 1474560 | tf_op jit(solution)/shard_map/reduce_scatter | solution.py:370
  564.7 26.6 %collective-permute-start.24 = (bf16[256,2304]{1,0:T(8,128)(2,1)S(1)}, bf16[256,2304]{1,0:T(8,128)(2,1)S(1)}, u32[]{:S(2)}, u32[]{:S(2)}) collective-permute-start(bf16[256,2304]{1,0:T(8,128)(2,1)S(1)} %fusion.7), channel_id=1, source_target_pairs={{0,2},{2,0},{1,3},{3,1},{4,6},{6,4},{5,7},{7,5},{8,10},{10,8},{9,1... | collective-permute-start | bytes 3538952 | tf_op jit(solution)/shard_map/ppermute | solution.py:334
  (154 other events, 1127.3 us)
Sparse Core Ops, SparseCore 0:
  258.1 17.6 reduce-scatter.22
  298.7 19.3 reduce-scatter.20
  336.0 17.4 reduce-scatter.12
  355.6 28.3 reduce-scatter.26
  386.2 27.8 reduce-scatter.24
  444.1 27.5 reduce-scatter.28
  494.9 27.1 reduce-scatter.18
  545.5 21.4 reduce-scatter.10
  569.3 28.3 reduce-scatter.16
  599.8 28.9 reduce-scatter.14
